TPU v7x, 32 devices: a whole 2x2x4 slice. The times are simulated.
32 devices in a mesh: groups: 2 (over x), tiles: 16 (over z, y, core).
Axes of the slice: x: 2, y: 2, z: 4, core: 2. Of those that a mesh axis runs over, the one named last changes fastest.
Arguments:
- video_q: bfloat16 [8192, 3072], P(('groups', 'tiles')), parts along dimension 0, may hold values from -88 to 88, as said below
- video_k: bfloat16 [8192, 3072], P(('groups', 'tiles')), parts along dimension 0, may hold values from -4 to 4, as said below
- video_v: bfloat16 [8192, 3072], P(('groups', 'tiles')), parts along dimension 0, may hold values from -5 to 5
- text_q: bfloat16 [512, 3072], P('groups'), parts along dimension 0, may hold values from -88 to 88
- text_k: bfloat16 [512, 3072], P('groups'), parts along dimension 0, may hold values from -5 to 5
- text_v: bfloat16 [512, 3072], P('groups'), parts along dimension 0, may hold values from -5 to 5
- window: int32 [32, 6], P('tiles'), may hold values from 0 to 13, as said below
- counts: int32 [64], P(('groups', 'tiles')), parts along dimension 0, may hold values from 1 to 128, as said below
- text_count: int32 [2], P('groups'), parts along dimension 0, may hold values from 64 to 256
Outputs:
- video_out: bfloat16 [8192, 3072], P(('groups', 'tiles')), parts along dimension 0
- text_out: bfloat16 [512, 3072], P(('groups', 'tiles')), parts along dimension 0
There are 2 independent parts, one for each index of `groups`. A program takes and returns all parts, laid end to end along the dimension named above; an argument that names none is the same for every part. Nothing has to cross between parts.
Inputs may be any that keep to these rules, and one draw needn't show every extreme that they name: `video_q`: queries drawn for the problem. `video_k`: keys drawn for the problem. `window`: each row names 6 different codes, among them always 3, 6, 9 and 12. `counts`: valid tokens are the first slots of a tile.
All inputs are finite; a program needn't handle non-finite values.
Results may differ from a plain program's by a relative error of at most 0.003.
Values may be sent and summed in bfloat16 or wider, within the bound.
A program may use at most 192 MiB of HBM per device.

v0:
```python
import functools
import math

import jax
import jax.numpy as jnp
from jax import lax
from jax.experimental import pallas as pl
from jax.experimental.pallas import tpu as pltpu
from jax.sharding import PartitionSpec as P

HEADS = 24
HD = 128
NR = 4
WIDTH = 256
LOG2E_SCALE = math.log2(math.e) / math.sqrt(HD)
MESH = pl.DeviceIdType.MESH
NT = (((1,), (1,)), ((), ()))


def main_kernel(
    n, q_ref, k_ref, v_ref, tq_ref, tk_ref, tv_ref, pick_ref, own_ref, qv_ref, tok_ref,
    out_ref, tout_ref,
    near, near_bias, relay, tnum, tstat, rnum, rstat,
    send_sem, recv_sem, bsend_sem, brecv_sem, fsend_sem, rsend_sem, rrecv_sem, tsend_sem, trecv_sem,
):
    group = lax.axis_index("groups")
    me = lax.axis_index("tiles")
    last = n // NR - 1
    chunks = q_ref.shape[1] // WIDTH
    per_chunk = WIDTH // HD
    tokens = q_ref.shape[0]
    half = tokens // 2
    share = tout_ref.shape[0]

    def at(offset):
        return lax.rem(me + offset + n, n)

    def time_of(index):
        return lax.div(lax.rem(index + n // 2 + NR + NR // 2, n), NR)

    row = lax.rem(me + n // 2 + NR + NR // 2, NR)
    time = time_of(me)
    side = lax.rem(me, 2)
    has = (time > 0, time < last, row > 0, row < NR - 1)
    offs = (-NR, NR, -1, 1)
    even = lax.rem(row, 2) == 0
    odd = lax.rem(row, 2) == 1
    quarter = lax.rem(me, 4)
    wrap_up = (quarter == 1) & (me < NR) & (time > 0)
    wrap_down = (quarter == 1) & (me >= n - NR) & (time < last)
    relay_up = (quarter == 3) & (me < NR) & (time_of(at(-2)) > 0)
    relay_down = (quarter == 3) & (me >= n - NR) & (time_of(at(-2)) < last)
    forward_down = (row == 1) & (time > 0)
    forward_up = (row == 2) & (time < last)

    barrier = pltpu.get_barrier_semaphore()

    def greet(i, _):
        pl.semaphore_signal(barrier, inc=1, device_id=(group, at(i)), device_id_type=MESH)
        return 0

    lax.fori_loop(1, n, greet, 0)
    pl.semaphore_wait(barrier, n - 1)

    def remote(source, target, sent, got, to):
        return pltpu.make_async_remote_copy(
            src_ref=source, dst_ref=target, send_sem=sent, recv_sem=got,
            device_id=(group, to), device_id_type=MESH,
        )

    def block(kv, c):
        cols = pl.ds(pl.multiple_of(c * WIDTH, WIDTH), WIDTH)
        return (k_ref, v_ref)[kv].at[:, cols]

    def bias_copy(d):
        return remote(own_ref, near_bias.at[d], bsend_sem.at[d], brecv_sem.at[d], at(-offs[d]))

    def direct(d, kv, c):
        return remote(
            block(kv, c), near.at[d, kv, c], send_sem.at[d, kv, c], recv_sem.at[d, kv, c], at(-offs[d])
        )

    def to_relay(d, kv, c):
        return remote(
            block(kv, c), relay.at[kv, c], send_sem.at[d, kv, c], rrecv_sem.at[kv, c], at(2)
        )

    def from_relay(d, kv, c):
        return remote(
            relay.at[kv, c], near.at[d, kv, c], rsend_sem.at[kv, c], recv_sem.at[d, kv, c],
            at(-2 - offs[d]),
        )

    def forward(d, kv, c):
        slot, to = (2, at(1 - NR)) if d == 0 else (3, at(NR - 1))
        return remote(
            near.at[d, kv, c], near.at[slot, kv, c], fsend_sem.at[kv, c], recv_sem.at[slot, kv, c], to
        )

    pair_sends = (((2, even), (0, 1)), ((3, odd), (0, 1)))
    far_sends = (
        ((0, (time < last) & jnp.logical_not(wrap_down)), (0, 1)),
        ((0, wrap_down), (1,)),
        ((1, (time > 0) & jnp.logical_not(wrap_up)), (0, 1)),
        ((2, (row == 1) & (time == last)), (0, 1)),
        ((3, (row == 2) & (time == 0)), (0, 1)),
    )
    relay_sends = (((0, wrap_down), (0,)), ((1, wrap_up), (0, 1)))
    onward = (((0, relay_down), (0,)), ((1, relay_up), (0, 1)))
    forwards = (((0, forward_down), (0, 1)), ((1, forward_up), (0, 1)))

    def each(table, make, act, c):
        for (d, when), kinds in table:
            @pl.when(when)
            def _(d=d, kinds=kinds):
                for kv in kinds:
                    act(make(d, kv, c))

    def start(copy):
        copy.start()

    def wait_send(copy):
        copy.wait_send()

    bias_sends = (has[1], has[0], has[3], has[2])
    for d in range(4):
        @pl.when(bias_sends[d])
        def _(d=d):
            bias_copy(d).start()

    def start_far(c, _):
        each(relay_sends, to_relay, start, c)
        each(far_sends, direct, start, c)

        def pass_on(d, kinds):
            for kv in kinds:
                pltpu.make_async_remote_copy(
                    src_ref=block(kv, c), dst_ref=relay.at[kv, c], send_sem=send_sem.at[d, kv, c],
                    recv_sem=rrecv_sem.at[kv, c], device_id=(group, at(2)), device_id_type=MESH,
                ).wait_recv()
                from_relay(d, kv, c).start()

        for (d, when), kinds in onward:
            @pl.when(when)
            def _(d=d, kinds=kinds):
                pass_on(d, kinds)
        return 0

    def start_pair(c, _):
        each(pair_sends, direct, start, c)
        return 0

    def missing(d):
        near_bias[d] = jnp.full(near_bias.shape[1:], -jnp.inf, jnp.float32)

        def clear(c, _):
            near[d, 0, c] = jnp.zeros(near.shape[3:], jnp.bfloat16)
            near[d, 1, c] = jnp.zeros(near.shape[3:], jnp.bfloat16)
            return 0

        lax.fori_loop(0, chunks, clear, 0)

    lax.fori_loop(0, 2, start_far, 0)
    lax.fori_loop(0, chunks, start_pair, 0)
    for d in range(4):
        @pl.when(jnp.logical_not(has[d]))
        def _(d=d):
            missing(d)

        @pl.when(has[d])
        def _(d=d):
            bias_copy(d).wait_recv()

    text_chunks = chunks // 2
    first = side * text_chunks
    lanes = lax.broadcasted_iota(jnp.int32, (share, 128), 1)

    def pair_arrived(c, _):
        for d, when in ((3, even), (2, odd)):
            @pl.when(when)
            def _(d=d):
                direct(d, 0, c).wait_recv()
                direct(d, 1, c).wait_recv()
        return 0

    lax.fori_loop(0, chunks, pair_arrived, 0)
    pair_slot = 3 - lax.rem(row, 2)
    tstat[...] = jnp.zeros_like(tstat)

    def text_part(j, _):
        c = first + j
        for h in range(per_chunk):
            cols = pl.ds(pl.multiple_of(c * WIDTH + h * HD, HD), HD)
            here = slice(h * HD, (h + 1) * HD)
            to = pl.ds(pl.multiple_of(j * WIDTH + h * HD, HD), HD)
            q = tq_ref[:, cols]
            s0 = lax.dot_general(q, k_ref[:, cols], NT, preferred_element_type=jnp.float32)
            s1 = lax.dot_general(
                q, near[pair_slot, 0, c, :, here], NT, preferred_element_type=jnp.float32
            )
            s0 = s0 + own_ref[0:1, :]
            s1 = s1 + near_bias[pair_slot, 0:1, :]
            top = jnp.max(jnp.maximum(s0, s1), axis=1, keepdims=True)
            p0 = jnp.exp2((s0 - top) * LOG2E_SCALE)
            p1 = jnp.exp2((s1 - top) * LOG2E_SCALE)
            total = jnp.sum(p0 + p1, axis=1, keepdims=True)
            num = None
            for p, value in ((p0, v_ref[:, cols]), (p1, near[pair_slot, 1, c, :, here])):
                wide = p * 65537.0
                high = wide - (wide - p)
                for part in (high, p - high):
                    term = jnp.dot(
                        part.astype(jnp.bfloat16), value, preferred_element_type=jnp.float32
                    )
                    num = term if num is None else num + term
            num = num.astype(jnp.bfloat16)
            head = j * per_chunk + h
            for b in range(n):
                rows = slice(b * share, (b + 1) * share)
                tnum[b, :, to] = num[rows]
                stat = jnp.where(lanes == head, top[rows], tstat[b])
                tstat[b] = jnp.where(lanes == head + 64, total[rows], stat)
        return 0

    lax.fori_loop(0, text_chunks, text_part, 0)

    def text_copies(i, there, here):
        return (
            remote(tnum.at[there], rnum.at[here], tsend_sem.at[0, i], trecv_sem.at[0, i], there),
            remote(tstat.at[there], rstat.at[here], tsend_sem.at[1, i], trecv_sem.at[1, i], there),
        )

    def start_text(i, _):
        for copy in text_copies(i, at(i), me):
            copy.start()
        return 0

    lax.fori_loop(1, n, start_text, 0)
    rnum[me] = tnum[me]
    rstat[me] = tstat[me]
    lax.fori_loop(2, chunks, start_far, 0)

    waits = (
        (0, has[0]), (1, has[1]),
        (2, has[2] & even), (3, has[3] & odd),
    )

    def attend(c, _):
        for d, when in waits[:2]:
            @pl.when(when)
            def _(d=d):
                direct(d, 0, c).wait_recv()
                direct(d, 1, c).wait_recv()
        each(forwards, forward, start, c)
        for d, when in waits[2:]:
            @pl.when(when)
            def _(d=d):
                direct(d, 0, c).wait_recv()
                direct(d, 1, c).wait_recv()
        for h in range(WIDTH // HD):
            cols = pl.ds(pl.multiple_of(c * WIDTH + h * HD, HD), HD)
            here = slice(h * HD, (h + 1) * HD)
            q = q_ref[:, cols]
            scores = []
            for b in range(6):
                if b == 0:
                    key, extra = k_ref[:, cols], own_ref[0:1, :]
                elif b == 5:
                    key, extra = tk_ref[:, cols], None
                else:
                    key, extra = near[b - 1, 0, c, :, here], near_bias[b - 1, 0:1, :]
                s = lax.dot_general(q, key, NT, preferred_element_type=jnp.float32)
                parts = []
                for t in range(2):
                    bias = pick_ref[b, t:t + 1, :]
                    if extra is not None:
                        bias = bias + extra
                    parts.append(s[t * half:(t + 1) * half] + bias)
                scores.append(jnp.concatenate(parts, axis=0))
            top = functools.reduce(jnp.maximum, scores)
            top = jnp.max(top, axis=1, keepdims=True)
            total, num = None, None
            for b in range(6):
                p = jnp.exp2((scores[b] - top) * LOG2E_SCALE)
                total = p if total is None else total + p
                if b == 0:
                    value = v_ref[:, cols]
                elif b == 5:
                    value = tv_ref[:, cols]
                else:
                    value = near[b - 1, 1, c, :, here]
                term = jnp.dot(p.astype(jnp.bfloat16), value, preferred_element_type=jnp.float32)
                num = term if num is None else num + term
            total = jnp.sum(total, axis=1, keepdims=True)
            result = jnp.where(qv_ref[...] > 0, num / total, 0.0)
            out_ref[:, cols] = result.astype(jnp.bfloat16)
        return 0

    lax.fori_loop(0, chunks, attend, 0)

    def finish(c, _):
        each(pair_sends, direct, wait_send, c)
        each(far_sends, direct, wait_send, c)
        each(relay_sends, to_relay, wait_send, c)
        each(onward, from_relay, wait_send, c)
        each(forwards, forward, wait_send, c)
        return 0

    def text_arrived(i, _):
        for copy in text_copies(i, at(n - i), at(n - i)):
            copy.wait_recv()
        for copy in text_copies(i, at(i), me):
            copy.wait_send()
        return 0

    lax.fori_loop(1, n, text_arrived, 0)

    heads = tnum.shape[2] // HD
    for e in range(2):
        top = lax.fori_loop(
            1, n // 2, lambda i, m: jnp.maximum(m, rstat[2 * i + e]), rstat[e]
        )

        def add(i, carry):
            den, nums = carry
            stat = rstat[2 * i + e]
            scale = jnp.exp2((stat - top) * LOG2E_SCALE)
            den = den + scale * jnp.roll(stat, 64, axis=1)
            nums = tuple(
                nums[j]
                + rnum[2 * i + e, :, j * HD:(j + 1) * HD].astype(jnp.float32) * scale[:, j:j + 1]
                for j in range(heads)
            )
            return den, nums

        zeros = jnp.zeros((share, HD), jnp.float32)
        den, nums = lax.fori_loop(0, n // 2, add, (zeros, (zeros,) * heads))
        for j in range(heads):
            result = jnp.where(tok_ref[...] > 0, nums[j] / den[:, j:j + 1], 0.0)
            at_head = (e * heads + j) * HD
            tout_ref[:, at_head:at_head + HD] = result.astype(jnp.bfloat16)

    for d in range(4):
        @pl.when(bias_sends[d])
        def _(d=d):
            bias_copy(d).wait_send()
    lax.fori_loop(0, chunks, finish, 0)


def per_device(video_q, video_k, video_v, text_q, text_k, text_v, window, counts, text_count):
    n = lax.axis_size("tiles")
    position = lax.axis_index("tiles")
    tiles = counts.shape[0]
    tokens, width = video_q.shape
    tok = tokens // tiles
    text = text_q.shape[0]
    share = text // n
    slots = jnp.arange(tok, dtype=jnp.int32)
    valid = (slots[None, :] < counts[:, None]).reshape(-1)
    own_bias = jnp.broadcast_to(jnp.where(valid, 0.0, -jnp.inf)[None, :], (8, tokens))
    codes = jnp.concatenate([jnp.ones((tiles, 1), jnp.int32), window + (window >= 1)], axis=1)
    column = jnp.arange(tiles, dtype=jnp.int32)[:, None] + codes % 3 - 1
    block_ids = jnp.arange(5, dtype=jnp.int32)[:, None, None, None]
    column_ids = jnp.arange(tiles, dtype=jnp.int32)[None, None, :, None]
    hit = jnp.any(
        (codes[None, :, None, :] // 3 == block_ids) & (column[None, :, None, :] == column_ids),
        axis=-1,
    )
    pick = jnp.broadcast_to(hit[..., None], (5, tiles, tiles, tok)).reshape(5, tiles, tokens)
    text_ok = jnp.arange(text, dtype=jnp.int32) < text_count[0]
    text_pick = jnp.broadcast_to(text_ok[None, None, :], (1, tiles, text))
    pick = jnp.where(jnp.concatenate([pick, text_pick], axis=0), 0.0, -jnp.inf)
    pick = jnp.pad(pick, ((0, 0), (0, 8 - tiles), (0, 0)))
    query_valid = valid.astype(jnp.float32)[:, None]

    row_ids = position * share + jnp.arange(share, dtype=jnp.int32)
    row_valid = (row_ids < text_count[0]).astype(jnp.float32)[:, None]
    vmem = pl.BlockSpec(memory_space=pltpu.VMEM)
    chunks = width // WIDTH
    dma = pltpu.SemaphoreType.DMA
    video_out, text_out = pl.pallas_call(
        functools.partial(main_kernel, n),
        out_shape=(
            jax.ShapeDtypeStruct((tokens, width), jnp.bfloat16),
            jax.ShapeDtypeStruct((share, width), jnp.bfloat16),
        ),
        in_specs=[vmem] * 10,
        out_specs=(vmem, vmem),
        scratch_shapes=[
            pltpu.VMEM((4, 2, chunks, tokens, WIDTH), jnp.bfloat16),
            pltpu.VMEM((4, 8, tokens), jnp.float32),
            pltpu.VMEM((2, chunks, tokens, WIDTH), jnp.bfloat16),
            pltpu.VMEM((n, share, width // 2), jnp.bfloat16),
            pltpu.VMEM((n, share, 128), jnp.float32),
            pltpu.VMEM((n, share, width // 2), jnp.bfloat16),
            pltpu.VMEM((n, share, 128), jnp.float32),
            dma((4, 2, chunks)),
            dma((4, 2, chunks)),
            dma((4,)),
            dma((4,)),
            dma((2, chunks)),
            dma((2, chunks)),
            dma((2, chunks)),
            dma((2, n)),
            dma((2, n)),
        ],
        compiler_params=pltpu.CompilerParams(
            collective_id=0, has_side_effects=True, vmem_limit_bytes=56 * 1024 * 1024
        ),
    )(
        video_q, video_k, video_v, text_q, text_k, text_v, pick, own_bias, query_valid, row_valid
    )
    return (video_out, text_out)


def solution(mesh):
    return jax.shard_map(
        per_device,
        mesh=mesh,
        in_specs=(
            P(("groups", "tiles"), None),
            P(("groups", "tiles"), None),
            P(("groups", "tiles"), None),
            P("groups", None),
            P("groups", None),
            P("groups", None),
            P("tiles", None),
            P(("groups", "tiles")),
            P("groups"),
        ),
        out_specs=(P(("groups", "tiles"), None), P(("groups", "tiles"), None)),
        check_vma=False,
    )
```

profile of v0, /device:TPU:8, one launch (start us, length us, event | category | flops | bytes accessed | tf_op | source)
XLA Modules:
  0.0 171.7 jit_solution(5628569773562264725)
XLA Ops:
  1.3 0.7 fusion.1
  2.0 0.7 fusion.3
  2.7 0.7 select_bitcast_fusion
  3.4 0.1 and_select_fusion.1
  3.6 0.1 and_reduce_fusion
  3.7 0.1 copy.13
  3.8 0.1 broadcast_in_dim.20
  4.0 0.6 broadcast_in_dim.28.own_ref
  4.6 0.6 fusion.tok_ref
  5.2 0.6 pad.5.pick_ref
  5.8 0.8 copy.15.qv_ref
  6.6 161.7 %shard_map.104 = (bf16[256,3072]{1,0:T(8,128)(2,1)}, bf16[16,3072]{1,0:T(8,128)(2,1)}) custom-call(bf16[256,3072]{1,0:T(8,128)(2,1)} %q_ref.1, bf16[256,3072]{1,0:T(8,128)(2,1)} %k_ref.1, bf16[256,3072]{1,0:T(8,128)(2,1)} %v_ref.1, bf16[256,3072]{1,0:T(8,128)(2,1)} %tq_ref.1, bf16[256,3072]{1,0:T(8,128)(2,1)} %tk_ref.1, bf16[256,3072]{1,0:T(8,128)(2,1)} %tv_ref.1, ...), custom_call_target="tpu_custom_call" | custom-call | tf_op jit(solution)/shard_map/pallas_call | solution.py:381
  168.3 0.0 copy-start
  168.3 2.7 %copy.19 = bf16[256,3072]{1,0:T(8,128)(2,1)} copy(bf16[256,3072]{1,0:T(8,128)(2,1)} %get-tuple-element.6) | data formatting | bytes 3145728
  171.0 0.0 copy-done
  171.0 0.6 copy.20
  (7 shorter events, 0.1 us)
Async XLA Ops:
  168.3 2.7 %copy-start = (bf16[16,3072]{1,0:T(8,128)(2,1)S(1)}, bf16[16,3072]{1,0:T(8,128)(2,1)}, u32[]{:S(2)}) copy-start(bf16[16,3072]{1,0:T(8,128)(2,1)} %get-tuple-element.7) | copy-start | bytes 294916
where the time goes:
time: 172 us
  Pallas kernels  162 us (94%)
  local copies, waits for them, and re-layouts  5.59 us (3%)
  other arithmetic  3 us (2%)
    pallas_call x1, Pallas kernels, per_device(): pl.pallas_call(functools.partial(main_kernel, n), out_shape=(jax.ShapeDty...  162 us

commit v1 on v0

v1 whole, which is shorter than its diff:
```python
import functools
import math

import jax
import jax.numpy as jnp
from jax import lax
from jax.experimental import pallas as pl
from jax.experimental.pallas import tpu as pltpu
from jax.sharding import PartitionSpec as P

HD = 128
NR = 4
WIDTH = 256
PER = WIDTH // HD
AHEAD = 4
LOG2E_SCALE = math.log2(math.e) / math.sqrt(HD)
MESH = pl.DeviceIdType.MESH
NT = (((1,), (1,)), ((), ()))
NEG = -jnp.inf


def softmax_block(q, blocks, half):
    scores = []
    for key, _, bias in blocks:
        s = lax.dot_general(q, key, NT, preferred_element_type=jnp.float32)
        scores.append(
            jnp.concatenate([s[:half] + bias[0:1, :], s[half:] + bias[1:2, :]], axis=0)
        )
    top = functools.reduce(jnp.maximum, scores)
    top = jnp.max(top, axis=1, keepdims=True)
    total, num = None, None
    for s, (_, value, _) in zip(scores, blocks):
        p = jnp.exp2((s - top) * LOG2E_SCALE)
        total = p if total is None else total + p
        term = jnp.dot(p.astype(jnp.bfloat16), value, preferred_element_type=jnp.float32)
        num = term if num is None else num + term
    return num / jnp.sum(total, axis=1, keepdims=True)


def main_kernel(
    n, fold,
    q_hbm, k_hbm, v_hbm, tq_hbm, tk_hbm, tv_hbm, window_ref, counts_ref, tcount_ref,
    out_ref, tout_ref,
    q_ref, k_ref, v_ref, tq_ref, tk_ref, tv_ref,
    own_ref, bias_ref, qv_ref, near, near_bias,
    relay, far_bias, far_q, side, far_out, back,
    tnum, tstat, ynum, ystat, snum, sstat, rnum, rstat,
    load_sem, send_sem, recv_sem, bsend_sem, brecv_sem, fsend_sem, rsend_sem, rrecv_sem,
    qsend_sem, qrecv_sem, xsend_sem, xrecv_sem, osend_sem, orecv_sem,
    ysend_sem, yrecv_sem, zsend_sem, zrecv_sem,
):
    group = lax.axis_index("groups")
    me = lax.axis_index("tiles")
    last = n // NR - 1
    tokens, width = q_hbm.shape
    chunks = width // WIDTH
    pairs = chunks // 2
    tiles = counts_ref.shape[0]
    tok = tokens // tiles
    half = tokens // 2
    share = tout_ref.shape[0]
    text = tq_hbm.shape[0]
    ahead = min(AHEAD, pairs)

    def at(offset):
        return lax.rem(me + offset + n, n)

    spot = lax.rem(me + n // 2 + NR + NR // 2, n)
    row = lax.rem(spot, NR)
    time = lax.div(spot, NR)
    core = lax.rem(me, 2)
    line = lax.rem(lax.div(me, 2), 2)
    has = (time > 0, time < last, row > 0, row < NR - 1)
    offs = (-NR, NR, -1, 1)
    even = lax.rem(row, 2) == 0
    odd = lax.rem(row, 2) == 1
    is_a = (me == 0) if fold else None
    is_b = (me == 1) if fold else None
    is_c = (me == n - 4) if fold else None
    is_d = (me == n - 3) if fold else None
    is_e = (me == n - 1) if fold else None

    barrier = pltpu.get_barrier_semaphore()

    def greet(i, _):
        pl.semaphore_signal(barrier, inc=1, device_id=(group, at(i)), device_id_type=MESH)
        return 0

    lax.fori_loop(1, n, greet, 0)

    loads = [
        pltpu.make_async_copy(source, target, load_sem.at[i])
        for i, (source, target) in enumerate((
            (k_hbm, k_ref), (tq_hbm, tq_ref), (v_hbm, v_ref),
            (q_hbm, q_ref), (tk_hbm, tk_ref), (tv_hbm, tv_ref),
        ))
    ]
    for copy in loads:
        copy.start()

    lane = lax.broadcasted_iota(jnp.int32, (8, tokens), 1)
    slot = lax.rem(lane, tok)
    count = jnp.full((8, tokens), counts_ref[0], jnp.int32)
    for s in range(1, tiles):
        count = jnp.where(lane >= s * tok, counts_ref[s], count)
    own_ref[...] = jnp.where(slot < count, 0.0, NEG)

    pl.semaphore_wait(barrier, n - 1)

    def remote(source, target, sent, got, to):
        return pltpu.make_async_remote_copy(
            src_ref=source, dst_ref=target, send_sem=sent, recv_sem=got,
            device_id=(group, to), device_id_type=MESH,
        )

    def columns(c):
        return pl.ds(pl.multiple_of(c * WIDTH, WIDTH), WIDTH)

    def block(kv, c):
        return (k_hbm, v_hbm)[kv].at[:, columns(c)]

    def bias_copy(d):
        return remote(own_ref, near_bias.at[d], bsend_sem.at[d], brecv_sem.at[d], at(-offs[d]))

    def direct(d, kv, c):
        return remote(
            block(kv, c), near.at[d, kv, c], send_sem.at[d, kv, c], recv_sem.at[d, kv, c], at(-offs[d])
        )

    def to_relay(d, kv, c):
        return remote(
            block(kv, c), relay.at[kv, c], send_sem.at[d, kv, c], rrecv_sem.at[kv, c], at(1 + kv)
        )

    def from_relay(d, kv, c):
        return remote(
            relay.at[kv, c], near.at[d, kv, c], rsend_sem.at[kv, c], recv_sem.at[d, kv, c],
            at(-1 - kv - offs[d]),
        )

    def forward(d, kv, c):
        slot, to = (2, at(1 - NR)) if d == 0 else (3, at(NR - 1))
        return remote(
            near.at[d, kv, c], near.at[slot, kv, c], fsend_sem.at[kv, c], recv_sem.at[slot, kv, c], to
        )

    def q_direct(j):
        return remote(
            q_hbm.at[:, columns(2 * j)], far_q.at[j], qsend_sem.at[j], qrecv_sem.at[j], at(-NR)
        )

    def q_to_relay(j):
        return remote(
            q_hbm.at[:, columns(2 * j)], relay.at[1, j], qsend_sem.at[j], rrecv_sem.at[1, j], at(2)
        )

    def q_from_relay(j):
        return remote(relay.at[1, j], far_q.at[j], rsend_sem.at[1, j], qrecv_sem.at[j], at(-2 - NR))

    def out_direct(j):
        return remote(far_out.at[j], back.at[j], osend_sem.at[j], orecv_sem.at[j], at(NR))

    def out_to_relay(j):
        return remote(far_out.at[j], relay.at[1, j], osend_sem.at[j], rrecv_sem.at[1, j], at(2))

    def out_from_relay(j):
        return remote(relay.at[1, j], back.at[j], rsend_sem.at[1, j], orecv_sem.at[j], at(2))

    def beside(kv, j):
        return remote(
            near.at[1, kv, 2 * j], side.at[0, kv, j], xsend_sem.at[kv, j], xrecv_sem.at[0, kv, j], at(-1)
        )

    def above(kv, j):
        return remote(
            block(kv, 2 * j), side.at[1, kv, j], xsend_sem.at[kv, j], xrecv_sem.at[1, kv, j], at(-3)
        )

    def far_bias_copy():
        return remote(bias_ref, far_bias, bsend_sem.at[4], brecv_sem.at[4], at(-NR))

    off = jnp.logical_not
    plain_next, plain_prev = time < last, time > 0
    plain_down = (row == 1) & (time == last)
    both = (0, 1)
    early, far, handed, slow, onward = [], [], [], [], []
    if fold:
        relays = ((me == 2) | (me == 3), me == n - 2)
        plain_next = plain_next & (me < n - NR) & off(relays[0])
        plain_prev = plain_prev & (me >= NR) & off(relays[1])
        plain_down = plain_down & off(is_e)
        early = [
            (direct, 0, is_c, both, False),
            (to_relay, 0, is_d, (0,), True),
            (direct, 0, is_d, (1,), True),
            (direct, 2, is_e, both, False),
        ]
        far = [(direct, 1, is_a, both, True)]
        handed = [(to_relay, 1, is_b, both, True)]
        slow = [(direct, 0, relays[0], both, True), (direct, 1, relays[1], both, True)]
        onward = [(me == 2, 1, (0,)), (me == 3, 1, (1,)), (me == n - 2, 0, (0,))]
    early = early + [
        (direct, 0, plain_next, both, True),
        (direct, 1, plain_prev, both, True),
        (direct, 2, plain_down, both, True),
        (direct, 3, (row == 2) & (time == 0), both, True),
    ]
    forwards = [(0, (row == 1) & (time > 0)), (1, (row == 2) & (time < last))]

    def when(condition, act):
        pl.when(condition)(act)

    def send_pair(sends, j, act):
        for o in range(2):
            c = 2 * j + o
            for make, d, condition, kinds, moved in sends:
                if o == 0 and not moved:
                    continue

                def go(make=make, d=d, kinds=kinds, c=c):
                    for kv in kinds:
                        act(make(d, kv, c))

                when(condition, go)
            if sends is far and fold and o == 0:
                @pl.when(is_a & (lax.rem(j, 2) == 0))
                def _():
                    act(q_direct(j))

                @pl.when(is_a & (lax.rem(j, 2) == 1))
                def _():
                    act(q_to_relay(j))

            if sends is early and fold and o == 0:
                @pl.when(is_e)
                def _():
                    act(above(0, j))
                    act(above(1, j))

    def pass_on(j):
        for o in range(2):
            c = 2 * j + o
            for condition, d, kinds in onward:
                @pl.when(condition)
                def _(d=d, kinds=kinds, c=c):
                    for kv in kinds:
                        to_relay(d, kv, c).wait_recv()
                        from_relay(d, kv, c).start()
        if fold:
            @pl.when((me == 2) & (lax.rem(j, 2) == 1))
            def _():
                q_to_relay(j).wait_recv()
                q_from_relay(j).start()

    def pass_pair(j):
        if fold:
            @pl.when(j < pairs)
            def _():
                pass_on(j)

            @pl.when(j + 1 < pairs)
            def _():
                send_pair(slow, j + 1, start)

    def pass_out(j):
        @pl.when((me == n - 2) & (lax.rem(j, 2) == 0))
        def _():
            out_to_relay(j).wait_recv()
            out_from_relay(j).start()

    def start(copy):
        copy.start()

    def wait_send(copy):
        copy.wait_send()

    bias_sends = (has[1], has[0], has[3], has[2])
    for d in range(4):
        @pl.when(bias_sends[d])
        def _(d=d):
            bias_copy(d).start()

    text_chunks = chunks // 2
    first = core * text_chunks

    def start_sibling(i, _):
        c = lax.rem((1 - core) * text_chunks + i, chunks)
        for d, condition in ((2, even), (3, odd)):
            @pl.when(condition)
            def _(d=d):
                direct(d, 0, c).start()
                direct(d, 1, c).start()
        return 0

    def start_pairs(sends, low, high):
        def go(j, _):
            send_pair(sends, j, start)
            return 0

        if sends and high > low:
            lax.fori_loop(low, high, go, 0)

    far_ahead, handed_ahead, passed = min(2, pairs), min(3, pairs), text_chunks // 2
    start_pairs(early, 0, 1)
    start_pairs(far, 0, 1)
    start_pairs(handed, 0, 1)
    start_pairs(slow, 0, 1)
    lax.fori_loop(0, chunks, start_sibling, 0)
    start_pairs(early, 1, ahead)
    start_pairs(far, 1, far_ahead)
    start_pairs(handed, 1, handed_ahead)

    def missing(d):
        near_bias[d] = jnp.full(near_bias.shape[1:], NEG, jnp.float32)

        def clear(c, _):
            near[d, 0, c] = jnp.zeros(near.shape[3:], jnp.bfloat16)
            near[d, 1, c] = jnp.zeros(near.shape[3:], jnp.bfloat16)
            return 0

        lax.fori_loop(0, chunks, clear, 0)

    for d in range(4):
        @pl.when(off(has[d]))
        def _(d=d):
            missing(d)

        @pl.when(has[d])
        def _(d=d):
            bias_copy(d).wait_recv()

    codes = []
    for t in range(tiles):
        found = []
        for i in range(window_ref.shape[1]):
            w = window_ref[t, i]
            found.append(w + jnp.where(w >= 1, 1, 0))
        codes.append(found)
    for b in range(5):
        for t in range(tiles):
            pick = jnp.zeros((8, tokens), jnp.int32)
            for s in range(tiles):
                want = 3 * b + s - t + 1
                if want == 1:
                    hits = jnp.int32(1)
                elif 3 * b <= want < 3 * b + 3:
                    hits = functools.reduce(
                        jnp.add, [jnp.where(e == want, 1, 0) for e in codes[t]]
                    )
                else:
                    hits = jnp.int32(0)
                pick = jnp.where((lane >= s * tok) & (lane < (s + 1) * tok), hits, pick)
            extra = own_ref[...] if b == 0 else near_bias[b - 1]
            total = jnp.where(pick > 0, 0.0, NEG) + extra
            bias_ref[b, t:t + 1, :] = total[0:1]
    text_lane = lax.broadcasted_iota(jnp.int32, (8, text), 1)
    bias_ref[5] = jnp.where(text_lane < tcount_ref[0], 0.0, NEG)
    if fold:
        @pl.when(is_a)
        def _():
            far_bias_copy().start()
    rows = lax.broadcasted_iota(jnp.int32, (tokens, HD), 0)
    limit = jnp.full((tokens, HD), counts_ref[0], jnp.int32)
    for s in range(1, tiles):
        limit = jnp.where(rows >= s * tok, counts_ref[s], limit)
    qv_ref[...] = jnp.where(lax.rem(rows, tok) < limit, 1.0, 0.0)

    lanes = lax.broadcasted_iota(jnp.int32, (share, 128), 1)
    tstat[...] = jnp.zeros_like(tstat)
    pair_slot = 3 - lax.rem(row, 2)

    def sibling_arrived(c):
        for d, condition in ((3, even), (2, odd)):
            @pl.when(condition)
            def _(d=d):
                direct(d, 0, c).wait_recv()
                direct(d, 1, c).wait_recv()

    for copy in loads[:3]:
        copy.wait()

    def text_part(j, _):
        c = first + j
        sibling_arrived(c)
        for h in range(PER):
            cols = pl.ds(pl.multiple_of(c * WIDTH + h * HD, HD), HD)
            here = slice(h * HD, (h + 1) * HD)
            to = pl.ds(pl.multiple_of(j * WIDTH + h * HD, HD), HD)
            q = tq_ref[:, cols]
            s0 = lax.dot_general(q, k_ref[:, cols], NT, preferred_element_type=jnp.float32)
            s1 = lax.dot_general(
                q, near[pair_slot, 0, c, :, here], NT, preferred_element_type=jnp.float32
            )
            s0 = s0 + own_ref[0:1, :]
            s1 = s1 + near_bias[pair_slot, 0:1, :]
            top = jnp.max(jnp.maximum(s0, s1), axis=1, keepdims=True)
            p0 = jnp.exp2((s0 - top) * LOG2E_SCALE)
            p1 = jnp.exp2((s1 - top) * LOG2E_SCALE)
            total = jnp.sum(p0 + p1, axis=1, keepdims=True)
            num = None
            for p, value in ((p0, v_ref[:, cols]), (p1, near[pair_slot, 1, c, :, here])):
                wide = p * 65537.0
                high = wide - (wide - p)
                for part in (high, p - high):
                    term = jnp.dot(
                        part.astype(jnp.bfloat16), value, preferred_element_type=jnp.float32
                    )
                    num = term if num is None else num + term
            head = j * PER + h
            for b in range(n):
                y, k = (b // 2) % 2, (b // 4) * 2 + b % 2
                part = slice(b * share, (b + 1) * share)
                tnum[y, k, :, to] = num[part]
                stat = jnp.where(lanes == head, top[part], tstat[y, k])
                tstat[y, k] = jnp.where(lanes == head + 64, total[part], stat)

        if fold:
            @pl.when(lax.rem(j, 2) == 1)
            def _():
                pass_pair(lax.div(j, 2))
        return 0

    lax.fori_loop(0, text_chunks, text_part, 0)

    partner = at(2 - 4 * line)

    def y_copies(there):
        return (
            remote(tnum.at[there], ynum, ysend_sem.at[0], yrecv_sem.at[0], partner),
            remote(tstat.at[there], ystat, ysend_sem.at[1], yrecv_sem.at[1], partner),
        )

    for copy in y_copies(1 - line):
        copy.start()
    start_pairs(handed, handed_ahead, pairs)

    peers = n // 2
    my_peer = lax.div(me, 4) * 2 + core
    heads = snum.shape[2] // HD

    def z_copies(i, there, here):
        k = lax.rem(my_peer + i, peers)
        to = lax.div(k, 2) * 4 + 2 * line + lax.rem(k, 2)
        source = k if there is None else there
        target = my_peer if here is None else here
        return (
            remote(snum.at[source], rnum.at[target], zsend_sem.at[0, i], zrecv_sem.at[0, i], to),
            remote(sstat.at[source], rstat.at[target], zsend_sem.at[1, i], zrecv_sem.at[1, i], to),
        )

    def text_exchange():
        for copy in y_copies(1 - line):
            copy.wait_recv()

        def combine(k, _):
            mine, theirs = tstat[line, k], ystat[k]
            top = jnp.maximum(mine, theirs)
            one = jnp.exp2((mine - top) * LOG2E_SCALE)
            two = jnp.exp2((theirs - top) * LOG2E_SCALE)
            den = one * jnp.roll(mine, 64, axis=1) + two * jnp.roll(theirs, 64, axis=1)
            sstat[k] = jnp.where(lanes < 64, top, jnp.roll(den, 64, axis=1))
            for h in range(heads):
                cols = slice(h * HD, (h + 1) * HD)
                num = tnum[line, k, :, cols] * one[:, h:h + 1] + ynum[k, :, cols] * two[:, h:h + 1]
                snum[k, :, cols] = num.astype(jnp.bfloat16)
            return 0

        lax.fori_loop(0, peers, combine, 0)

        def start_z(i, _):
            for copy in z_copies(i, None, None):
                copy.start()
            return 0

        lax.fori_loop(1, peers, start_z, 0)
        start_pairs(early, ahead, pairs)
        rnum[my_peer] = snum[my_peer]
        rstat[my_peer] = sstat[my_peer]

    row_ids = me * share + lax.broadcasted_iota(jnp.int32, (share, HD), 0)
    row_valid = row_ids < jnp.full((share, HD), tcount_ref[0], jnp.int32)

    def text_finish():
        def arrived(i, _):
            for copy in z_copies(i, None, None):
                copy.wait_send()
                copy.wait_recv()
            return 0

        lax.fori_loop(1, peers, arrived, 0)
        for e in range(2):
            top = lax.fori_loop(
                1, peers // 2, lambda i, m: jnp.maximum(m, rstat[2 * i + e]), rstat[e]
            )

            def add(i, carry):
                den, nums = carry
                stat = rstat[2 * i + e]
                scale = jnp.exp2((stat - top) * LOG2E_SCALE)
                den = den + scale * jnp.roll(stat, 64, axis=1)
                nums = tuple(
                    nums[j]
                    + rnum[2 * i + e, :, j * HD:(j + 1) * HD].astype(jnp.float32) * scale[:, j:j + 1]
                    for j in range(heads)
                )
                return den, nums

            zeros = jnp.zeros((share, HD), jnp.float32)
            den, nums = lax.fori_loop(0, peers // 2, add, (zeros, (zeros,) * heads))
            for j in range(heads):
                result = jnp.where(row_valid, nums[j] / den[:, j:j + 1], 0.0)
                at_head = (e * heads + j) * HD
                tout_ref[:, at_head:at_head + HD] = result.astype(jnp.bfloat16)

    def rest_arrived(i, _):
        sibling_arrived(lax.rem(first + text_chunks + i, chunks))
        return 0

    lax.fori_loop(0, chunks - text_chunks, rest_arrived, 0)
    for copy in loads[3:]:
        copy.wait()

    def got(d, c, condition, moved):
        @pl.when(condition & off(is_a) if fold and moved else condition)
        def _():
            direct(d, 0, c).wait_recv()
            direct(d, 1, c).wait_recv()

    def arrive(j, c, moved):
        for d in range(2):
            got(d, c, has[d], moved)
            for source, condition in forwards:
                if source == d:
                    @pl.when(condition)
                    def _(d=d):
                        forward(d, 0, c).start()
                        forward(d, 1, c).start()
        if fold and moved:
            @pl.when(is_d)
            def _():
                beside(0, j).start()
                beside(1, j).start()

    def attend(j, c, moved):
        skip = is_a if (fold and moved) else None
        got(2, c, has[2] & even, moved)
        got(3, c, has[3] & odd, moved)

        def mine():
            for h in range(PER):
                cols = pl.ds(pl.multiple_of(c * WIDTH + h * HD, HD), HD)
                here = slice(h * HD, (h + 1) * HD)
                blocks = [(k_ref[:, cols], v_ref[:, cols], bias_ref.at[0])]
                for d in range(4):
                    blocks.append((near[d, 0, c, :, here], near[d, 1, c, :, here], bias_ref.at[d + 1]))
                blocks.append((tk_ref[:, cols], tv_ref[:, cols], bias_ref.at[5]))
                result = softmax_block(q_ref[:, cols], blocks, half)
                out_ref[:, cols] = jnp.where(qv_ref[...] > 0, result, 0.0).astype(jnp.bfloat16)

        if skip is None:
            mine()
        else:
            pl.when(off(skip))(mine)

        if fold and moved:
            @pl.when(is_c)
            def _():
                @pl.when(j == 0)
                def _():
                    far_bias_copy().wait_recv()

                q_direct(j).wait_recv()
                for kv in range(2):
                    beside(kv, j).wait_recv()
                    above(kv, j).wait_recv()
                for h in range(PER):
                    cols = pl.ds(pl.multiple_of(c * WIDTH + h * HD, HD), HD)
                    here = slice(h * HD, (h + 1) * HD)
                    blocks = [
                        (near[1, 0, c, :, here], near[1, 1, c, :, here], far_bias.at[0]),
                        (k_ref[:, cols], v_ref[:, cols], far_bias.at[1]),
                        (side[1, 0, j, :, here], side[1, 1, j, :, here], far_bias.at[3]),
                        (side[0, 0, j, :, here], side[0, 1, j, :, here], far_bias.at[4]),
                        (tk_ref[:, cols], tv_ref[:, cols], far_bias.at[5]),
                    ]
                    result = softmax_block(far_q[j, :, here], blocks, half)
                    far_out[j, :, here] = result.astype(jnp.bfloat16)

                @pl.when(lax.rem(j, 2) == 0)
                def _():
                    out_to_relay(j).start()

                @pl.when(lax.rem(j, 2) == 1)
                def _():
                    out_direct(j).start()

    def step(j, _):
        if fold:
            @pl.when(j + far_ahead < pairs)
            def _():
                send_pair(far, j + far_ahead, start)

        arrive(j, 2 * j + 1, False)
        attend(j, 2 * j, True)

        @pl.when(j + 1 < pairs)
        def _():
            arrive(j + 1, 2 * j + 2, True)

        attend(j, 2 * j + 1, False)

        if fold:
            pass_pair(j + passed)

            @pl.when(j > 0)
            def _():
                pass_out(j - 1)

        @pl.when(j == min(1, pairs - 1))
        def _():
            text_exchange()

        @pl.when(j == pairs - 2)
        def _():
            text_finish()
        return 0

    arrive(jnp.int32(0), jnp.int32(0), True)
    lax.fori_loop(0, pairs, step, 0)

    if fold:
        pass_out(jnp.int32(pairs - 1))

        @pl.when(is_a)
        def _():
            def take(j, _):
                out_direct(j).wait_recv()
                for h in range(PER):
                    cols = pl.ds(pl.multiple_of(2 * j * WIDTH + h * HD, HD), HD)
                    result = back[j, :, h * HD:(h + 1) * HD].astype(jnp.float32)
                    out_ref[:, cols] = jnp.where(qv_ref[...] > 0, result, 0.0).astype(jnp.bfloat16)
                return 0

            lax.fori_loop(0, pairs, take, 0)

    for d in range(4):
        @pl.when(bias_sends[d])
        def _(d=d):
            bias_copy(d).wait_send()
    for copy in y_copies(1 - line):
        copy.wait_send()

    def finish(j, _):
        for sends in (early, far, handed, slow):
            send_pair(sends, j, wait_send)
        for o in range(2):
            c = 2 * j + o
            for d, condition in ((2, even), (3, odd)):
                @pl.when(condition)
                def _(d=d, c=c):
                    direct(d, 0, c).wait_send()
                    direct(d, 1, c).wait_send()
            for condition, d, kinds in onward:
                @pl.when(condition)
                def _(d=d, kinds=kinds, c=c):
                    for kv in kinds:
                        from_relay(d, kv, c).wait_send()
            for d, condition in forwards:
                @pl.when(condition)
                def _(d=d, c=c):
                    forward(d, 0, c).wait_send()
                    forward(d, 1, c).wait_send()
        if fold:
            @pl.when((me == 2) & (lax.rem(j, 2) == 1))
            def _():
                q_from_relay(j).wait_send()

            @pl.when((me == n - 2) & (lax.rem(j, 2) == 0))
            def _():
                out_from_relay(j).wait_send()

            @pl.when(is_c)
            def _():
                out_direct(j).wait_send()

            @pl.when(is_d)
            def _():
                beside(0, j).wait_send()
                beside(1, j).wait_send()
        return 0

    lax.fori_loop(0, pairs, finish, 0)
    if fold:
        @pl.when(is_a)
        def _():
            far_bias_copy().wait_send()


def per_device(video_q, video_k, video_v, text_q, text_k, text_v, window, counts, text_count):
    n = lax.axis_size("tiles")
    tokens, width = video_q.shape
    text = text_q.shape[0]
    share = text // n
    chunks = width // WIDTH
    pairs = chunks // 2
    peers = n // 2
    fold = n // 2 + NR + NR // 2 == n - 2
    vmem = pl.BlockSpec(memory_space=pltpu.VMEM)
    smem = pl.BlockSpec(memory_space=pltpu.SMEM)
    hbm = pl.BlockSpec(memory_space=pl.ANY)
    dma = pltpu.SemaphoreType.DMA
    bf16, f32 = jnp.bfloat16, jnp.float32
    block = (tokens, WIDTH)
    video_out, text_out = pl.pallas_call(
        functools.partial(main_kernel, n, fold),
        out_shape=(
            jax.ShapeDtypeStruct((tokens, width), bf16),
            jax.ShapeDtypeStruct((share, width), bf16),
        ),
        in_specs=[hbm] * 6 + [smem] * 3,
        out_specs=(vmem, vmem),
        scratch_shapes=[
            *[pltpu.VMEM((tokens, width), bf16)] * 3,
            *[pltpu.VMEM((text, width), bf16)] * 3,
            pltpu.VMEM((8, tokens), f32),
            pltpu.VMEM((6, 8, tokens), f32),
            pltpu.VMEM((tokens, HD), f32),
            pltpu.VMEM((4, 2, chunks, *block), bf16),
            pltpu.VMEM((4, 8, tokens), f32),
            pltpu.VMEM((2, chunks, *block), bf16),
            pltpu.VMEM((6, 8, tokens), f32),
            pltpu.VMEM((pairs, *block), bf16),
            pltpu.VMEM((2, 2, pairs, *block), bf16),
            pltpu.VMEM((pairs, *block), bf16),
            pltpu.VMEM((pairs, *block), bf16),
            pltpu.VMEM((2, peers, share, width // 2), f32),
            pltpu.VMEM((2, peers, share, 128), f32),
            pltpu.VMEM((peers, share, width // 2), f32),
            pltpu.VMEM((peers, share, 128), f32),
            pltpu.VMEM((peers, share, width // 2), bf16),
            pltpu.VMEM((peers, share, 128), f32),
            pltpu.VMEM((peers, share, width // 2), bf16),
            pltpu.VMEM((peers, share, 128), f32),
            dma((6,)),
            dma((4, 2, chunks)),
            dma((4, 2, chunks)),
            dma((5,)),
            dma((5,)),
            dma((2, chunks)),
            dma((2, chunks)),
            dma((2, chunks)),
            dma((pairs,)),
            dma((pairs,)),
            dma((2, pairs)),
            dma((2, 2, pairs)),
            dma((pairs,)),
            dma((pairs,)),
            dma((2,)),
            dma((2,)),
            dma((2, peers)),
            dma((2, peers)),
        ],
        compiler_params=pltpu.CompilerParams(
            collective_id=0, has_side_effects=True, vmem_limit_bytes=56 * 1024 * 1024
        ),
    )(video_q, video_k, video_v, text_q, text_k, text_v, window, counts, text_count)
    return (video_out, text_out)


def solution(mesh):
    return jax.shard_map(
        per_device,
        mesh=mesh,
        in_specs=(
            P(("groups", "tiles"), None),
            P(("groups", "tiles"), None),
            P(("groups", "tiles"), None),
            P("groups", None),
            P("groups", None),
            P("groups", None),
            P("tiles", None),
            P(("groups", "tiles")),
            P("groups"),
        ),
        out_specs=(P(("groups", "tiles"), None), P(("groups", "tiles"), None)),
        check_vma=False,
    )
```

time: 172 us -> 152 us (0.88)
  the two profiles are of different devices: /device:TPU:8 before, /device:TPU:0 now
where the time goes in v1:
time: 152 us
  Pallas kernels  148 us (97%)
  local copies, waits for them, and re-layouts  3.33 us (2%)
    pallas_call x1, Pallas kernels, per_device(): pl.pallas_call(functools.partial(main_kernel, n, fold), out_shape=(jax.Sh...  148 us
    unnamed x4, local copies, waits for them, and re-layouts  3.33 us

profile of v1, /device:TPU:0, one launch (start us, length us, event | category | flops | bytes accessed | tf_op | source)
XLA Modules:
  0.0 152.2 jit_solution(9538223025514067251)
XLA Ops:
  1.3 147.6 %shard_map.104 = (bf16[256,3072]{1,0:T(8,128)(2,1)}, bf16[16,3072]{1,0:T(8,128)(2,1)}) custom-call(bf16[256,3072]{1,0:T(8,128)(2,1)} %q_hbm.1, bf16[256,3072]{1,0:T(8,128)(2,1)} %k_hbm.1, bf16[256,3072]{1,0:T(8,128)(2,1)} %v_hbm.1, bf16[256,3072]{1,0:T(8,128)(2,1)} %tq_hbm.1, bf16[256,3072]{1,0:T(8,128)(2,1)} %tk_hbm.1, bf16[256,3072]{1,0:T(8,128)(2,1)} %tv_hbm.1, ...), custom_call_target="tpu_custom_call" | custom-call | tf_op jit(solution)/shard_map/pallas_call | solution.py:714
  148.9 0.0 copy-start
  148.9 2.7 %copy.14 = bf16[256,3072]{1,0:T(8,128)(2,1)} copy(bf16[256,3072]{1,0:T(8,128)(2,1)} %get-tuple-element.4) | data formatting | bytes 3145728
  151.6 0.0 copy-done
  151.6 0.6 copy.15
Async XLA Ops:
  148.9 2.7 %copy-start = (bf16[16,3072]{1,0:T(8,128)(2,1)S(1)}, bf16[16,3072]{1,0:T(8,128)(2,1)}, u32[]{:S(2)}) copy-start(bf16[16,3072]{1,0:T(8,128)(2,1)} %get-tuple-element.5) | copy-start | bytes 294916

commit v2 on v1

--- a/solution.py
+++ b/solution.py
@@ -45,7 +45,7 @@
     own_ref, bias_ref, qv_ref, near, near_bias,
     relay, far_bias, far_q, side, far_out, back,
     tnum, tstat, ynum, ystat, snum, sstat, rnum, rstat,
-    load_sem, send_sem, recv_sem, bsend_sem, brecv_sem, fsend_sem, rsend_sem, rrecv_sem,
+    load_sem, send_sem, recv_sem, bsend_sem, brecv_sem, fsend_sem, hsend_sem, rsend_sem, rrecv_sem,
     qsend_sem, qrecv_sem, xsend_sem, xrecv_sem, osend_sem, orecv_sem,
     ysend_sem, yrecv_sem, zsend_sem, zrecv_sem,
 ):
@@ -129,13 +129,14 @@
 
     def to_relay(d, kv, c):
         return remote(
-            block(kv, c), relay.at[kv, c], send_sem.at[d, kv, c], rrecv_sem.at[kv, c], at(1 + kv)
+            block(kv, c), relay.at[kv, c], send_sem.at[d, kv, c], rrecv_sem.at[kv, c],
+            at(2 + kv if d == 3 else 1),
         )
 
     def from_relay(d, kv, c):
         return remote(
             relay.at[kv, c], near.at[d, kv, c], rsend_sem.at[kv, c], recv_sem.at[d, kv, c],
-            at(-1 - kv - offs[d]),
+            at(-3 - kv if d == 3 else 3),
         )
 
     def forward(d, kv, c):
@@ -146,7 +147,7 @@
 
     def q_direct(j):
         return remote(
-            q_hbm.at[:, columns(2 * j)], far_q.at[j], qsend_sem.at[j], qrecv_sem.at[j], at(-NR)
+            q_hbm.at[:, columns(2 * j)], far_q.at[j], qsend_sem.at[j], qrecv_sem.at[j], at(-1)
         )
 
     def q_to_relay(j):
@@ -155,29 +156,28 @@
         )
 
     def q_from_relay(j):
-        return remote(relay.at[1, j], far_q.at[j], rsend_sem.at[1, j], qrecv_sem.at[j], at(-2 - NR))
-
-    def out_direct(j):
-        return remote(far_out.at[j], back.at[j], osend_sem.at[j], orecv_sem.at[j], at(NR))
-
-    def out_to_relay(j):
-        return remote(far_out.at[j], relay.at[1, j], osend_sem.at[j], rrecv_sem.at[1, j], at(2))
-
-    def out_from_relay(j):
-        return remote(relay.at[1, j], back.at[j], rsend_sem.at[1, j], orecv_sem.at[j], at(2))
+        return remote(relay.at[1, j], far_q.at[j], rsend_sem.at[1, j], qrecv_sem.at[j], at(-3))
+
+    def out_copy(j):
+        return remote(far_out.at[j], back.at[j], osend_sem.at[j], orecv_sem.at[j], at(1))
+
+    def after(kv, c):
+        return remote(
+            near.at[3, kv, c], near.at[1, kv, c], hsend_sem.at[kv, c], recv_sem.at[1, kv, c], at(-3)
+        )
 
     def beside(kv, j):
         return remote(
-            near.at[1, kv, 2 * j], side.at[0, kv, j], xsend_sem.at[kv, j], xrecv_sem.at[0, kv, j], at(-1)
-        )
-
-    def above(kv, j):
-        return remote(
-            block(kv, 2 * j), side.at[1, kv, j], xsend_sem.at[kv, j], xrecv_sem.at[1, kv, j], at(-3)
+            near.at[1, kv, 2 * j], side.at[0, kv, j], xsend_sem.at[kv, j], xrecv_sem.at[0, kv, j], at(2)
+        )
+
+    def before(kv, j):
+        return remote(
+            block(kv, 2 * j), side.at[1, kv, j], xsend_sem.at[kv, j], xrecv_sem.at[1, kv, j], at(3)
         )
 
     def far_bias_copy():
-        return remote(bias_ref, far_bias, bsend_sem.at[4], brecv_sem.at[4], at(-NR))
+        return remote(bias_ref, far_bias, bsend_sem.at[4], brecv_sem.at[4], at(-1))
 
     off = jnp.logical_not
     plain_next, plain_prev = time < last, time > 0
@@ -190,67 +190,78 @@
         plain_prev = plain_prev & (me >= NR) & off(relays[1])
         plain_down = plain_down & off(is_e)
         early = [
-            (direct, 0, is_c, both, False),
-            (to_relay, 0, is_d, (0,), True),
-            (direct, 0, is_d, (1,), True),
-            (direct, 2, is_e, both, False),
+            (direct, 0, is_c, both, (1,)),
+            (to_relay, 0, is_d, (0,), (0, 2)),
+            (direct, 0, is_d, (0,), (3,)),
+            (direct, 0, is_d, (1,), (0, 1)),
+            (direct, 2, is_e, both, (1,)),
         ]
-        far = [(direct, 1, is_a, both, True)]
-        handed = [(to_relay, 1, is_b, both, True)]
-        slow = [(direct, 0, relays[0], both, True), (direct, 1, relays[1], both, True)]
-        onward = [(me == 2, 1, (0,)), (me == 3, 1, (1,)), (me == n - 2, 0, (0,))]
+        far = [(direct, 1, is_b, both, (0, 1))]
+        handed = [(to_relay, 3, is_a, both, (0, 1))]
+        slow = [(direct, 0, relays[0], both, (0, 1)), (direct, 1, relays[1], both, (0, 1))]
+        onward = [
+            (from_relay, 3, me == 2, (0,), (0, 1)),
+            (from_relay, 3, me == 3, (1,), (0, 1)),
+            (from_relay, 0, me == n - 2, (0,), (0, 2)),
+        ]
     early = early + [
-        (direct, 0, plain_next, both, True),
-        (direct, 1, plain_prev, both, True),
-        (direct, 2, plain_down, both, True),
-        (direct, 3, (row == 2) & (time == 0), both, True),
+        (direct, 0, plain_next, both, (0, 1)),
+        (direct, 1, plain_prev, both, (0, 1)),
+        (direct, 2, plain_down, both, (0, 1)),
     ]
-    forwards = [(0, (row == 1) & (time > 0)), (1, (row == 2) & (time < last))]
+    late = [(direct, 3, (row == 2) & (time == 0), both, (0, 1))]
+    carries = (row == 2) & (time < last)
+    forwards = [(0, (row == 1) & (time > 0)), (1, carries & off(is_c) if fold else carries)]
 
     def when(condition, act):
         pl.when(condition)(act)
 
     def send_pair(sends, j, act):
+        turn = lax.rem(j, 2)
         for o in range(2):
             c = 2 * j + o
-            for make, d, condition, kinds, moved in sends:
-                if o == 0 and not moved:
+            for make, d, condition, kinds, which in sends:
+                if o == 0 and 0 not in which or o == 1 and which == (0,):
                     continue
+                if o == 1 and 1 not in which:
+                    condition = condition & (turn == (0 if 2 in which else 1))
 
                 def go(make=make, d=d, kinds=kinds, c=c):
                     for kv in kinds:
                         act(make(d, kv, c))
 
                 when(condition, go)
-            if sends is far and fold and o == 0:
-                @pl.when(is_a & (lax.rem(j, 2) == 0))
+            if sends is handed and fold and o == 0:
+                @pl.when(is_a & (turn == 1))
                 def _():
                     act(q_direct(j))
 
-                @pl.when(is_a & (lax.rem(j, 2) == 1))
+                @pl.when(is_a & (turn == 0))
                 def _():
                     act(q_to_relay(j))
 
             if sends is early and fold and o == 0:
-                @pl.when(is_e)
+                @pl.when(is_c)
                 def _():
-                    act(above(0, j))
-                    act(above(1, j))
+                    act(before(0, j))
+                    act(before(1, j))
 
     def pass_on(j):
         for o in range(2):
             c = 2 * j + o
-            for condition, d, kinds in onward:
+            for make, d, condition, kinds, which in onward:
+                if o == 1 and 1 not in which:
+                    condition = condition & (lax.rem(j, 2) == 0)
+
                 @pl.when(condition)
                 def _(d=d, kinds=kinds, c=c):
                     for kv in kinds:
                         to_relay(d, kv, c).wait_recv()
                         from_relay(d, kv, c).start()
-        if fold:
-            @pl.when((me == 2) & (lax.rem(j, 2) == 1))
-            def _():
-                q_to_relay(j).wait_recv()
-                q_from_relay(j).start()
+        @pl.when((me == 2) & (lax.rem(j, 2) == 0))
+        def _():
+            q_to_relay(j).wait_recv()
+            q_from_relay(j).start()
 
     def pass_pair(j):
         if fold:
@@ -261,12 +272,6 @@
             @pl.when(j + 1 < pairs)
             def _():
                 send_pair(slow, j + 1, start)
-
-    def pass_out(j):
-        @pl.when((me == n - 2) & (lax.rem(j, 2) == 0))
-        def _():
-            out_to_relay(j).wait_recv()
-            out_from_relay(j).start()
 
     def start(copy):
         copy.start()
@@ -433,6 +438,7 @@
     for copy in y_copies(1 - line):
         copy.start()
     start_pairs(handed, handed_ahead, pairs)
+    start_pairs(late, 0, 1)
 
     peers = n // 2
     my_peer = lax.div(me, 4) * 2 + core
@@ -526,15 +532,23 @@
             direct(d, 0, c).wait_recv()
             direct(d, 1, c).wait_recv()
 
+    first_at = has[1] & off(is_c) if fold else has[1]
+
     def arrive(j, c, moved):
-        for d in range(2):
-            got(d, c, has[d], moved)
-            for source, condition in forwards:
+        for d, condition in ((0, has[0]), (1, first_at)):
+            got(d, c, condition, moved)
+            for source, sends in forwards:
                 if source == d:
-                    @pl.when(condition)
+                    @pl.when(sends)
                     def _(d=d):
                         forward(d, 0, c).start()
                         forward(d, 1, c).start()
+        if fold:
+            @pl.when(is_e)
+            def _():
+                for kv in range(2):
+                    direct(3, kv, c).wait_recv()
+                    after(kv, c).start()
         if fold and moved:
             @pl.when(is_d)
             def _():
@@ -543,8 +557,10 @@
 
     def attend(j, c, moved):
         skip = is_a if (fold and moved) else None
+        if fold:
+            got(1, c, is_c, False)
         got(2, c, has[2] & even, moved)
-        got(3, c, has[3] & odd, moved)
+        got(3, c, has[3] & odd & off(is_e) if fold else has[3] & odd, moved)
 
         def mine():
             for h in range(PER):
@@ -563,7 +579,7 @@
             pl.when(off(skip))(mine)
 
         if fold and moved:
-            @pl.when(is_c)
+            @pl.when(is_e)
             def _():
                 @pl.when(j == 0)
                 def _():
@@ -572,27 +588,20 @@
                 q_direct(j).wait_recv()
                 for kv in range(2):
                     beside(kv, j).wait_recv()
-                    above(kv, j).wait_recv()
+                    before(kv, j).wait_recv()
                 for h in range(PER):
                     cols = pl.ds(pl.multiple_of(c * WIDTH + h * HD, HD), HD)
                     here = slice(h * HD, (h + 1) * HD)
                     blocks = [
-                        (near[1, 0, c, :, here], near[1, 1, c, :, here], far_bias.at[0]),
-                        (k_ref[:, cols], v_ref[:, cols], far_bias.at[1]),
-                        (side[1, 0, j, :, here], side[1, 1, j, :, here], far_bias.at[3]),
+                        (near[3, 0, c, :, here], near[3, 1, c, :, here], far_bias.at[0]),
+                        (side[1, 0, j, :, here], side[1, 1, j, :, here], far_bias.at[1]),
+                        (k_ref[:, cols], v_ref[:, cols], far_bias.at[3]),
                         (side[0, 0, j, :, here], side[0, 1, j, :, here], far_bias.at[4]),
                         (tk_ref[:, cols], tv_ref[:, cols], far_bias.at[5]),
                     ]
                     result = softmax_block(far_q[j, :, here], blocks, half)
                     far_out[j, :, here] = result.astype(jnp.bfloat16)
-
-                @pl.when(lax.rem(j, 2) == 0)
-                def _():
-                    out_to_relay(j).start()
-
-                @pl.when(lax.rem(j, 2) == 1)
-                def _():
-                    out_direct(j).start()
+                out_copy(j).start()
 
     def step(j, _):
         if fold:
@@ -600,6 +609,10 @@
             def _():
                 send_pair(far, j + far_ahead, start)
 
+        @pl.when(j + 1 < pairs)
+        def _():
+            send_pair(late, j + 1, start)
+
         arrive(j, 2 * j + 1, False)
         attend(j, 2 * j, True)
 
@@ -612,10 +625,6 @@
         if fold:
             pass_pair(j + passed)
 
-            @pl.when(j > 0)
-            def _():
-                pass_out(j - 1)
-
         @pl.when(j == min(1, pairs - 1))
         def _():
             text_exchange()
@@ -629,12 +638,10 @@
     lax.fori_loop(0, pairs, step, 0)
 
     if fold:
-        pass_out(jnp.int32(pairs - 1))
-
         @pl.when(is_a)
         def _():
             def take(j, _):
-                out_direct(j).wait_recv()
+                out_copy(j).wait_recv()
                 for h in range(PER):
                     cols = pl.ds(pl.multiple_of(2 * j * WIDTH + h * HD, HD), HD)
                     result = back[j, :, h * HD:(h + 1) * HD].astype(jnp.float32)
@@ -651,8 +658,9 @@
         copy.wait_send()
 
     def finish(j, _):
-        for sends in (early, far, handed, slow):
+        for sends in (early, far, handed, slow, late):
             send_pair(sends, j, wait_send)
+        send_pair(onward, j, wait_send)
         for o in range(2):
             c = 2 * j + o
             for d, condition in ((2, even), (3, odd)):
@@ -660,28 +668,22 @@
                 def _(d=d, c=c):
                     direct(d, 0, c).wait_send()
                     direct(d, 1, c).wait_send()
-            for condition, d, kinds in onward:
-                @pl.when(condition)
-                def _(d=d, kinds=kinds, c=c):
-                    for kv in kinds:
-                        from_relay(d, kv, c).wait_send()
             for d, condition in forwards:
                 @pl.when(condition)
                 def _(d=d, c=c):
                     forward(d, 0, c).wait_send()
                     forward(d, 1, c).wait_send()
         if fold:
-            @pl.when((me == 2) & (lax.rem(j, 2) == 1))
+            @pl.when((me == 2) & (lax.rem(j, 2) == 0))
             def _():
                 q_from_relay(j).wait_send()
 
-            @pl.when((me == n - 2) & (lax.rem(j, 2) == 0))
-            def _():
-                out_from_relay(j).wait_send()
-
-            @pl.when(is_c)
-            def _():
-                out_direct(j).wait_send()
+            @pl.when(is_e)
+            def _():
+                out_copy(j).wait_send()
+                for o in range(2):
+                    after(0, 2 * j + o).wait_send()
+                    after(1, 2 * j + o).wait_send()
 
             @pl.when(is_d)
             def _():
@@ -749,6 +751,7 @@
             dma((2, chunks)),
             dma((2, chunks)),
             dma((2, chunks)),
+            dma((2, chunks)),
             dma((pairs,)),
             dma((pairs,)),
             dma((2, pairs)),

time: 152 us -> 141 us (0.928)
  the two profiles are of different devices: /device:TPU:0 before, /device:TPU:24 now
where the time goes in v2:
time: 141 us; the launch traced here: 139 us
  Pallas kernels  135 us (96%)
  local copies, waits for them, and re-layouts  3.33 us (2%)
    pallas_call x1, Pallas kernels, per_device(): pl.pallas_call(functools.partial(main_kernel, n, fold), out_shape=(jax.Sh...  135 us
    unnamed x4, local copies, waits for them, and re-layouts  3.33 us

profile of v2, /device:TPU:24, one launch (start us, length us, event | category | flops | bytes accessed | tf_op | source)
XLA Modules:
  0.0 139.3 jit_solution(3846500965684690976)
XLA Ops:
  1.3 134.7 %shard_map.104 = (bf16[256,3072]{1,0:T(8,128)(2,1)}, bf16[16,3072]{1,0:T(8,128)(2,1)}) custom-call(bf16[256,3072]{1,0:T(8,128)(2,1)} %q_hbm.1, bf16[256,3072]{1,0:T(8,128)(2,1)} %k_hbm.1, bf16[256,3072]{1,0:T(8,128)(2,1)} %v_hbm.1, bf16[256,3072]{1,0:T(8,128)(2,1)} %tq_hbm.1, bf16[256,3072]{1,0:T(8,128)(2,1)} %tk_hbm.1, bf16[256,3072]{1,0:T(8,128)(2,1)} %tv_hbm.1, ...), custom_call_target="tpu_custom_call" | custom-call | tf_op jit(solution)/shard_map/pallas_call | solution.py:716
  136.0 0.0 copy-start
  136.0 2.7 %copy.14 = bf16[256,3072]{1,0:T(8,128)(2,1)} copy(bf16[256,3072]{1,0:T(8,128)(2,1)} %get-tuple-element.4) | data formatting | bytes 3145728
  138.7 0.0 copy-done
  138.7 0.6 copy.15
Async XLA Ops:
  136.0 2.7 %copy-start = (bf16[16,3072]{1,0:T(8,128)(2,1)S(1)}, bf16[16,3072]{1,0:T(8,128)(2,1)}, u32[]{:S(2)}) copy-start(bf16[16,3072]{1,0:T(8,128)(2,1)} %get-tuple-element.5) | copy-start | bytes 294916

commit v3 on v2

--- a/solution.py
+++ b/solution.py
@@ -12,7 +12,7 @@
 NR = 4
 WIDTH = 256
 PER = WIDTH // HD
-AHEAD = 4
+AHEAD = 5
 LOG2E_SCALE = math.log2(math.e) / math.sqrt(HD)
 MESH = pl.DeviceIdType.MESH
 NT = (((1,), (1,)), ((), ()))
@@ -40,14 +40,14 @@
 def main_kernel(
     n, fold,
     q_hbm, k_hbm, v_hbm, tq_hbm, tk_hbm, tv_hbm, window_ref, counts_ref, tcount_ref,
-    out_ref, tout_ref,
-    q_ref, k_ref, v_ref, tq_ref, tk_ref, tv_ref,
+    out_hbm, tout_hbm,
+    out_ref, tout_ref, q_ref, k_ref, v_ref, tq_ref, tk_ref, tv_ref,
     own_ref, bias_ref, qv_ref, near, near_bias,
     relay, far_bias, far_q, side, far_out, back,
     tnum, tstat, ynum, ystat, snum, sstat, rnum, rstat,
     load_sem, send_sem, recv_sem, bsend_sem, brecv_sem, fsend_sem, hsend_sem, rsend_sem, rrecv_sem,
     qsend_sem, qrecv_sem, xsend_sem, xrecv_sem, osend_sem, orecv_sem,
-    ysend_sem, yrecv_sem, zsend_sem, zrecv_sem,
+    ysend_sem, yrecv_sem, zsend_sem, zrecv_sem, store_sem,
 ):
     group = lax.axis_index("groups")
     me = lax.axis_index("tiles")
@@ -130,13 +130,13 @@
     def to_relay(d, kv, c):
         return remote(
             block(kv, c), relay.at[kv, c], send_sem.at[d, kv, c], rrecv_sem.at[kv, c],
-            at(2 + kv if d == 3 else 1),
+            at(2 if d == 3 else 1),
         )
 
     def from_relay(d, kv, c):
         return remote(
             relay.at[kv, c], near.at[d, kv, c], rsend_sem.at[kv, c], recv_sem.at[d, kv, c],
-            at(-3 - kv if d == 3 else 3),
+            at(-3 if d == 3 else 3),
         )
 
     def forward(d, kv, c):
@@ -145,18 +145,21 @@
             near.at[d, kv, c], near.at[slot, kv, c], fsend_sem.at[kv, c], recv_sem.at[slot, kv, c], to
         )
 
+    def moved_chunk(i):
+        return jnp.maximum(2 * i - 1, 0)
+
     def q_direct(j):
         return remote(
-            q_hbm.at[:, columns(2 * j)], far_q.at[j], qsend_sem.at[j], qrecv_sem.at[j], at(-1)
+            q_hbm.at[:, columns(moved_chunk(j))], far_q.at[j], qsend_sem.at[j], qrecv_sem.at[j], at(-1)
         )
 
     def q_to_relay(j):
         return remote(
-            q_hbm.at[:, columns(2 * j)], relay.at[1, j], qsend_sem.at[j], rrecv_sem.at[1, j], at(2)
+            q_hbm.at[:, columns(moved_chunk(j))], relay.at[2, j], qsend_sem.at[j], rrecv_sem.at[2, j], at(2)
         )
 
     def q_from_relay(j):
-        return remote(relay.at[1, j], far_q.at[j], rsend_sem.at[1, j], qrecv_sem.at[j], at(-3))
+        return remote(relay.at[2, j], far_q.at[j], rsend_sem.at[2, j], qrecv_sem.at[j], at(-3))
 
     def out_copy(j):
         return remote(far_out.at[j], back.at[j], osend_sem.at[j], orecv_sem.at[j], at(1))
@@ -168,12 +171,12 @@
 
     def beside(kv, j):
         return remote(
-            near.at[1, kv, 2 * j], side.at[0, kv, j], xsend_sem.at[kv, j], xrecv_sem.at[0, kv, j], at(2)
+            near.at[1, kv, moved_chunk(j)], side.at[0, kv, j], xsend_sem.at[kv, j], xrecv_sem.at[0, kv, j], at(2)
         )
 
     def before(kv, j):
         return remote(
-            block(kv, 2 * j), side.at[1, kv, j], xsend_sem.at[kv, j], xrecv_sem.at[1, kv, j], at(3)
+            block(kv, moved_chunk(j)), side.at[1, kv, j], xsend_sem.at[kv, j], xrecv_sem.at[1, kv, j], at(3)
         )
 
     def far_bias_copy():
@@ -183,33 +186,39 @@
     plain_next, plain_prev = time < last, time > 0
     plain_down = (row == 1) & (time == last)
     both = (0, 1)
+    always, never = (lambda j: None), (lambda j: False)
+    every = (always, always)
+    moved = ((lambda j: j == 0), (lambda j: j < pairs - 1))
+    kept = ((lambda j: j > 0), (lambda j: j == pairs - 1))
+    relayed = (always, lambda j: lax.rem(j, 2) == 0)
+    unrelayed = (never, lambda j: lax.rem(j, 2) == 1)
     early, far, handed, slow, onward = [], [], [], [], []
     if fold:
-        relays = ((me == 2) | (me == 3), me == n - 2)
+        relays = (me == 2, me == n - 2)
         plain_next = plain_next & (me < n - NR) & off(relays[0])
         plain_prev = plain_prev & (me >= NR) & off(relays[1])
         plain_down = plain_down & off(is_e)
         early = [
-            (direct, 0, is_c, both, (1,)),
-            (to_relay, 0, is_d, (0,), (0, 2)),
-            (direct, 0, is_d, (0,), (3,)),
-            (direct, 0, is_d, (1,), (0, 1)),
-            (direct, 2, is_e, both, (1,)),
+            (direct, 0, is_c, both, kept),
+            (to_relay, 0, is_d, (0,), relayed),
+            (direct, 0, is_d, (0,), unrelayed),
+            (direct, 0, is_d, (1,), every),
+            (direct, 2, is_e, both, kept),
         ]
-        far = [(direct, 1, is_b, both, (0, 1))]
-        handed = [(to_relay, 3, is_a, both, (0, 1))]
-        slow = [(direct, 0, relays[0], both, (0, 1)), (direct, 1, relays[1], both, (0, 1))]
+        far = [(direct, 1, is_b, both, every)]
+        handed = [(to_relay, 3, is_a, both, every)]
+        slow = [(direct, 0, relays[0], both, every), (direct, 1, relays[1], both, every)]
         onward = [
-            (from_relay, 3, me == 2, (0,), (0, 1)),
-            (from_relay, 3, me == 3, (1,), (0, 1)),
-            (from_relay, 0, me == n - 2, (0,), (0, 2)),
+            (from_relay, 3, me == 2, both, every),
+            (from_relay, 0, me == n - 2, (0,), relayed),
         ]
     early = early + [
-        (direct, 0, plain_next, both, (0, 1)),
-        (direct, 1, plain_prev, both, (0, 1)),
-        (direct, 2, plain_down, both, (0, 1)),
+        (direct, 0, plain_next, both, every),
+        (direct, 1, plain_prev & (row < NR - 1), both, every),
+        (direct, 2, plain_down, both, every),
     ]
-    late = [(direct, 3, (row == 2) & (time == 0), both, (0, 1))]
+    calm = [(direct, 1, plain_prev & (row == NR - 1), both, every)]
+    late = [(direct, 3, (row == 2) & (time == 0), both, every)]
     carries = (row == 2) & (time < last)
     forwards = [(0, (row == 1) & (time > 0)), (1, carries & off(is_c) if fold else carries)]
 
@@ -217,61 +226,63 @@
         pl.when(condition)(act)
 
     def send_pair(sends, j, act):
-        turn = lax.rem(j, 2)
         for o in range(2):
             c = 2 * j + o
             for make, d, condition, kinds, which in sends:
-                if o == 0 and 0 not in which or o == 1 and which == (0,):
+                only = which[o](j)
+                if only is False:
                     continue
-                if o == 1 and 1 not in which:
-                    condition = condition & (turn == (0 if 2 in which else 1))
+                if only is not None:
+                    condition = condition & only
 
                 def go(make=make, d=d, kinds=kinds, c=c):
                     for kv in kinds:
                         act(make(d, kv, c))
 
                 when(condition, go)
-            if sends is handed and fold and o == 0:
-                @pl.when(is_a & (turn == 1))
-                def _():
-                    act(q_direct(j))
-
-                @pl.when(is_a & (turn == 0))
-                def _():
-                    act(q_to_relay(j))
-
-            if sends is early and fold and o == 0:
-                @pl.when(is_c)
-                def _():
-                    act(before(0, j))
-                    act(before(1, j))
+            i = j + o
+            if sends is handed and fold:
+                @pl.when(is_a & moved[o](j))
+                def _(i=i):
+                    @pl.when(lax.rem(i, 2) == 1)
+                    def _():
+                        act(q_direct(i))
+
+                    @pl.when(lax.rem(i, 2) == 0)
+                    def _():
+                        act(q_to_relay(i))
+
+            if sends is early and fold:
+                @pl.when(is_c & moved[o](j))
+                def _(i=i):
+                    act(before(0, i))
+                    act(before(1, i))
 
     def pass_on(j):
         for o in range(2):
             c = 2 * j + o
             for make, d, condition, kinds, which in onward:
-                if o == 1 and 1 not in which:
-                    condition = condition & (lax.rem(j, 2) == 0)
+                only = which[o](j)
+                if only is not None:
+                    condition = condition & only
 
                 @pl.when(condition)
-                def _(d=d, kinds=kinds, c=c):
+                def _(make=make, d=d, kinds=kinds, c=c):
                     for kv in kinds:
                         to_relay(d, kv, c).wait_recv()
-                        from_relay(d, kv, c).start()
-        @pl.when((me == 2) & (lax.rem(j, 2) == 0))
-        def _():
-            q_to_relay(j).wait_recv()
-            q_from_relay(j).start()
+                        make(d, kv, c).start()
+
+            @pl.when((me == 2) & moved[o](j) & (lax.rem(j + o, 2) == 0))
+            def _(i=j + o):
+                q_to_relay(i).wait_recv()
+                q_from_relay(i).start()
 
     def pass_pair(j):
         if fold:
             @pl.when(j < pairs)
             def _():
                 pass_on(j)
-
-            @pl.when(j + 1 < pairs)
-            def _():
-                send_pair(slow, j + 1, start)
+                send_pair(slow, j, start)
 
     def start(copy):
         copy.start()
@@ -309,7 +320,6 @@
     start_pairs(early, 0, 1)
     start_pairs(far, 0, 1)
     start_pairs(handed, 0, 1)
-    start_pairs(slow, 0, 1)
     lax.fori_loop(0, chunks, start_sibling, 0)
     start_pairs(early, 1, ahead)
     start_pairs(far, 1, far_ahead)
@@ -438,6 +448,7 @@
     for copy in y_copies(1 - line):
         copy.start()
     start_pairs(handed, handed_ahead, pairs)
+    start_pairs(calm, 0, ahead)
     start_pairs(late, 0, 1)
 
     peers = n // 2
@@ -480,6 +491,7 @@
 
         lax.fori_loop(1, peers, start_z, 0)
         start_pairs(early, ahead, pairs)
+        start_pairs(calm, ahead, pairs)
         rnum[my_peer] = snum[my_peer]
         rstat[my_peer] = sstat[my_peer]
 
@@ -517,6 +529,7 @@
                 result = jnp.where(row_valid, nums[j] / den[:, j:j + 1], 0.0)
                 at_head = (e * heads + j) * HD
                 tout_ref[:, at_head:at_head + HD] = result.astype(jnp.bfloat16)
+        text_stored.start()
 
     def rest_arrived(i, _):
         sibling_arrived(lax.rem(first + text_chunks + i, chunks))
@@ -526,41 +539,53 @@
     for copy in loads[3:]:
         copy.wait()
 
-    def got(d, c, condition, moved):
-        @pl.when(condition & off(is_a) if fold and moved else condition)
-        def _():
-            direct(d, 0, c).wait_recv()
-            direct(d, 1, c).wait_recv()
-
-    first_at = has[1] & off(is_c) if fold else has[1]
-
-    def arrive(j, c, moved):
-        for d, condition in ((0, has[0]), (1, first_at)):
-            got(d, c, condition, moved)
-            for source, sends in forwards:
-                if source == d:
-                    @pl.when(sends)
-                    def _(d=d):
-                        forward(d, 0, c).start()
-                        forward(d, 1, c).start()
+    def stored(c):
+        return pltpu.make_async_copy(
+            out_ref.at[:, columns(c)], out_hbm.at[:, columns(c)], store_sem.at[c]
+        )
+
+    text_stored = pltpu.make_async_copy(tout_ref, tout_hbm, store_sem.at[chunks])
+
+    hands0, hands1 = forwards[0][1], forwards[1][1]
+    if fold:
+        hands1 = hands1 | is_d
+
+    def arrive(j, o):
+        c = 2 * j + o
+        for d, condition in forwards:
+            @pl.when(condition)
+            def _(d=d):
+                for kv in range(2):
+                    direct(d, kv, c).wait_recv()
+                    forward(d, kv, c).start()
         if fold:
+            @pl.when(is_d)
+            def _():
+                for kv in range(2):
+                    direct(1, kv, c).wait_recv()
+
+                    @pl.when(moved[o](j))
+                    def _(kv=kv):
+                        beside(kv, j + o).start()
+
             @pl.when(is_e)
             def _():
                 for kv in range(2):
                     direct(3, kv, c).wait_recv()
                     after(kv, c).start()
-        if fold and moved:
-            @pl.when(is_d)
-            def _():
-                beside(0, j).start()
-                beside(1, j).start()
-
-    def attend(j, c, moved):
-        skip = is_a if (fold and moved) else None
-        if fold:
-            got(1, c, is_c, False)
-        got(2, c, has[2] & even, moved)
-        got(3, c, has[3] & odd & off(is_e) if fold else has[3] & odd, moved)
+
+    def attend(j, o):
+        c = 2 * j + o
+        skip = is_a & moved[o](j) if fold else None
+        awaited = [
+            (0, has[0] & off(hands0)), (1, has[1] & off(hands1)),
+            (2, has[2] & even), (3, has[3] & odd & off(is_e) if fold else has[3] & odd),
+        ]
+        for d, condition in awaited:
+            @pl.when(condition if skip is None or d % 2 else condition & off(skip))
+            def _(d=d):
+                direct(d, 0, c).wait_recv()
+                direct(d, 1, c).wait_recv()
 
         def mine():
             for h in range(PER):
@@ -572,93 +597,50 @@
                 blocks.append((tk_ref[:, cols], tv_ref[:, cols], bias_ref.at[5]))
                 result = softmax_block(q_ref[:, cols], blocks, half)
                 out_ref[:, cols] = jnp.where(qv_ref[...] > 0, result, 0.0).astype(jnp.bfloat16)
+            stored(c).start()
 
         if skip is None:
             mine()
         else:
             pl.when(off(skip))(mine)
 
-        if fold and moved:
-            @pl.when(is_e)
-            def _():
-                @pl.when(j == 0)
+        if fold:
+            @pl.when(is_e & moved[o](j))
+            def _(i=j + o):
+                @pl.when(i == 0)
                 def _():
                     far_bias_copy().wait_recv()
 
-                q_direct(j).wait_recv()
+                q_direct(i).wait_recv()
                 for kv in range(2):
-                    beside(kv, j).wait_recv()
-                    before(kv, j).wait_recv()
+                    beside(kv, i).wait_recv()
+                    before(kv, i).wait_recv()
                 for h in range(PER):
                     cols = pl.ds(pl.multiple_of(c * WIDTH + h * HD, HD), HD)
                     here = slice(h * HD, (h + 1) * HD)
                     blocks = [
                         (near[3, 0, c, :, here], near[3, 1, c, :, here], far_bias.at[0]),
-                        (side[1, 0, j, :, here], side[1, 1, j, :, here], far_bias.at[1]),
+                        (side[1, 0, i, :, here], side[1, 1, i, :, here], far_bias.at[1]),
                         (k_ref[:, cols], v_ref[:, cols], far_bias.at[3]),
-                        (side[0, 0, j, :, here], side[0, 1, j, :, here], far_bias.at[4]),
+                        (side[0, 0, i, :, here], side[0, 1, i, :, here], far_bias.at[4]),
                         (tk_ref[:, cols], tv_ref[:, cols], far_bias.at[5]),
                     ]
-                    result = softmax_block(far_q[j, :, here], blocks, half)
-                    far_out[j, :, here] = result.astype(jnp.bfloat16)
-                out_copy(j).start()
-
-    def step(j, _):
-        if fold:
-            @pl.when(j + far_ahead < pairs)
-            def _():
-                send_pair(far, j + far_ahead, start)
-
-        @pl.when(j + 1 < pairs)
-        def _():
-            send_pair(late, j + 1, start)
-
-        arrive(j, 2 * j + 1, False)
-        attend(j, 2 * j, True)
-
-        @pl.when(j + 1 < pairs)
-        def _():
-            arrive(j + 1, 2 * j + 2, True)
-
-        attend(j, 2 * j + 1, False)
-
-        if fold:
-            pass_pair(j + passed)
-
-        @pl.when(j == min(1, pairs - 1))
-        def _():
-            text_exchange()
-
-        @pl.when(j == pairs - 2)
-        def _():
-            text_finish()
-        return 0
-
-    arrive(jnp.int32(0), jnp.int32(0), True)
-    lax.fori_loop(0, pairs, step, 0)
-
-    if fold:
+                    result = softmax_block(far_q[i, :, here], blocks, half)
+                    far_out[i, :, here] = result.astype(jnp.bfloat16)
+                out_copy(i).start()
+
+    def take(j):
         @pl.when(is_a)
         def _():
-            def take(j, _):
-                out_copy(j).wait_recv()
-                for h in range(PER):
-                    cols = pl.ds(pl.multiple_of(2 * j * WIDTH + h * HD, HD), HD)
-                    result = back[j, :, h * HD:(h + 1) * HD].astype(jnp.float32)
-                    out_ref[:, cols] = jnp.where(qv_ref[...] > 0, result, 0.0).astype(jnp.bfloat16)
-                return 0
-
-            lax.fori_loop(0, pairs, take, 0)
-
-    for d in range(4):
-        @pl.when(bias_sends[d])
-        def _(d=d):
-            bias_copy(d).wait_send()
-    for copy in y_copies(1 - line):
-        copy.wait_send()
-
-    def finish(j, _):
-        for sends in (early, far, handed, slow, late):
+            out_copy(j).wait_recv()
+            for h in range(PER):
+                cols = pl.ds(pl.multiple_of(moved_chunk(j) * WIDTH + h * HD, HD), HD)
+                result = back[j, :, h * HD:(h + 1) * HD].astype(jnp.float32)
+                out_ref[:, cols] = jnp.where(qv_ref[...] > 0, result, 0.0).astype(jnp.bfloat16)
+            stored(moved_chunk(j)).start()
+
+    def finish(j):
+        for sends in (early, calm, far, handed, slow, late):
             send_pair(sends, j, wait_send)
         send_pair(onward, j, wait_send)
         for o in range(2):
@@ -689,9 +671,72 @@
             def _():
                 beside(0, j).wait_send()
                 beside(1, j).wait_send()
+
+    def step(j, _):
+        if fold:
+            @pl.when(j + far_ahead < pairs)
+            def _():
+                send_pair(far, j + far_ahead, start)
+
+        @pl.when(j + 1 < pairs)
+        def _():
+            send_pair(late, j + 1, start)
+
+        arrive(j, 1)
+        attend(j, 0)
+
+        @pl.when(j + 1 < pairs)
+        def _():
+            arrive(j + 1, 0)
+
+        attend(j, 1)
+
+        @pl.when(j > 2)
+        def _():
+            finish(j - 3)
+
+        if fold:
+            pass_pair(j + passed)
+
+            @pl.when(j == 1)
+            def _():
+                take(0)
+
+            @pl.when(j > 0)
+            def _():
+                take(j)
+
+        @pl.when(j == min(1, pairs - 1))
+        def _():
+            text_exchange()
+
+        @pl.when(j == pairs - 2)
+        def _():
+            text_finish()
         return 0
 
-    lax.fori_loop(0, pairs, finish, 0)
+    arrive(jnp.int32(0), 0)
+    lax.fori_loop(0, pairs, step, 0)
+
+    def stores(c, _):
+        stored(c).wait()
+        return 0
+
+    lax.fori_loop(0, chunks, stores, 0)
+    text_stored.wait()
+
+    for d in range(4):
+        @pl.when(bias_sends[d])
+        def _(d=d):
+            bias_copy(d).wait_send()
+    for copy in y_copies(1 - line):
+        copy.wait_send()
+
+    def finish_rest(j, _):
+        finish(j)
+        return 0
+
+    lax.fori_loop(max(pairs - 3, 0), pairs, finish_rest, 0)
     if fold:
         @pl.when(is_a)
         def _():
@@ -707,7 +752,6 @@
     pairs = chunks // 2
     peers = n // 2
     fold = n // 2 + NR + NR // 2 == n - 2
-    vmem = pl.BlockSpec(memory_space=pltpu.VMEM)
     smem = pl.BlockSpec(memory_space=pltpu.SMEM)
     hbm = pl.BlockSpec(memory_space=pl.ANY)
     dma = pltpu.SemaphoreType.DMA
@@ -720,8 +764,10 @@
             jax.ShapeDtypeStruct((share, width), bf16),
         ),
         in_specs=[hbm] * 6 + [smem] * 3,
-        out_specs=(vmem, vmem),
+        out_specs=(hbm, hbm),
         scratch_shapes=[
+            pltpu.VMEM((tokens, width), bf16),
+            pltpu.VMEM((share, width), bf16),
             *[pltpu.VMEM((tokens, width), bf16)] * 3,
             *[pltpu.VMEM((text, width), bf16)] * 3,
             pltpu.VMEM((8, tokens), f32),
@@ -729,7 +775,7 @@
             pltpu.VMEM((tokens, HD), f32),
             pltpu.VMEM((4, 2, chunks, *block), bf16),
             pltpu.VMEM((4, 8, tokens), f32),
-            pltpu.VMEM((2, chunks, *block), bf16),
+            pltpu.VMEM((3, chunks, *block), bf16),
             pltpu.VMEM((6, 8, tokens), f32),
             pltpu.VMEM((pairs, *block), bf16),
             pltpu.VMEM((2, 2, pairs, *block), bf16),
@@ -750,8 +796,8 @@
             dma((5,)),
             dma((2, chunks)),
             dma((2, chunks)),
-            dma((2, chunks)),
-            dma((2, chunks)),
+            dma((3, chunks)),
+            dma((3, chunks)),
             dma((pairs,)),
             dma((pairs,)),
             dma((2, pairs)),
@@ -762,6 +808,7 @@
             dma((2,)),
             dma((2, peers)),
             dma((2, peers)),
+            dma((chunks + 1,)),
         ],
         compiler_params=pltpu.CompilerParams(
             collective_id=0, has_side_effects=True, vmem_limit_bytes=56 * 1024 * 1024

time: 141 us -> 136 us (0.965)
  Pallas kernels: 135 us -> 130 us
    pallas_call x1, Pallas kernels: 135 us -> 130 us  [per_device(): pl.pallas_call(functools.partial(main_kernel, n, fold), out_shape=(jax.Sh...]
where the time goes in v3:
time: 136 us; the launch traced here: 135 us
  Pallas kernels  130 us (96%)
  local copies, waits for them, and re-layouts  3.33 us (2%)
    pallas_call x1, Pallas kernels, per_device(): pl.pallas_call(functools.partial(main_kernel, n, fold), out_shape=(jax.Sh...  130 us
    unnamed x4, local copies, waits for them, and re-layouts  3.33 us

profile of v3, /device:TPU:24, one launch (start us, length us, event | category | flops | bytes accessed | tf_op | source)
XLA Modules:
  0.0 134.6 jit_solution(1019889205121606974)
XLA Ops:
  1.3 130.0 %shard_map.104 = (bf16[256,3072]{1,0:T(8,128)(2,1)}, bf16[16,3072]{1,0:T(8,128)(2,1)}) custom-call(bf16[256,3072]{1,0:T(8,128)(2,1)} %q_hbm.1, bf16[256,3072]{1,0:T(8,128)(2,1)} %k_hbm.1, bf16[256,3072]{1,0:T(8,128)(2,1)} %v_hbm.1, bf16[256,3072]{1,0:T(8,128)(2,1)} %tq_hbm.1, bf16[256,3072]{1,0:T(8,128)(2,1)} %tk_hbm.1, bf16[256,3072]{1,0:T(8,128)(2,1)} %tv_hbm.1, ...), custom_call_target="tpu_custom_call" | custom-call | tf_op jit(solution)/shard_map/pallas_call | solution.py:760
  131.3 0.0 copy-start
  131.3 2.7 %copy.14 = bf16[256,3072]{1,0:T(8,128)(2,1)} copy(bf16[256,3072]{1,0:T(8,128)(2,1)} %get-tuple-element.4) | data formatting | bytes 3145728
  134.0 0.0 copy-done
  134.0 0.6 copy.15
Async XLA Ops:
  131.3 2.7 %copy-start = (bf16[16,3072]{1,0:T(8,128)(2,1)S(1)}, bf16[16,3072]{1,0:T(8,128)(2,1)}, u32[]{:S(2)}) copy-start(bf16[16,3072]{1,0:T(8,128)(2,1)} %get-tuple-element.5) | copy-start | bytes 294916

commit v4 on v3

--- a/solution.py
+++ b/solution.py
@@ -13,6 +13,7 @@
 WIDTH = 256
 PER = WIDTH // HD
 AHEAD = 5
+PARTS = 8
 LOG2E_SCALE = math.log2(math.e) / math.sqrt(HD)
 MESH = pl.DeviceIdType.MESH
 NT = (((1,), (1,)), ((), ()))
@@ -192,13 +193,13 @@
     kept = ((lambda j: j > 0), (lambda j: j == pairs - 1))
     relayed = (always, lambda j: lax.rem(j, 2) == 0)
     unrelayed = (never, lambda j: lax.rem(j, 2) == 1)
-    early, far, handed, slow, onward = [], [], [], [], []
+    leading, far, handed, slow, onward = [], [], [], [], []
     if fold:
         relays = (me == 2, me == n - 2)
         plain_next = plain_next & (me < n - NR) & off(relays[0])
         plain_prev = plain_prev & (me >= NR) & off(relays[1])
         plain_down = plain_down & off(is_e)
-        early = [
+        leading = [
             (direct, 0, is_c, both, kept),
             (to_relay, 0, is_d, (0,), relayed),
             (direct, 0, is_d, (0,), unrelayed),
@@ -212,7 +213,7 @@
             (from_relay, 3, me == 2, both, every),
             (from_relay, 0, me == n - 2, (0,), relayed),
         ]
-    early = early + [
+    early = [
         (direct, 0, plain_next, both, every),
         (direct, 1, plain_prev & (row < NR - 1), both, every),
         (direct, 2, plain_down, both, every),
@@ -317,11 +318,14 @@
             lax.fori_loop(low, high, go, 0)
 
     far_ahead, handed_ahead, passed = min(2, pairs), min(3, pairs), text_chunks // 2
+    start_pairs(leading, 0, min(2, pairs))
     start_pairs(early, 0, 1)
     start_pairs(far, 0, 1)
     start_pairs(handed, 0, 1)
     lax.fori_loop(0, chunks, start_sibling, 0)
-    start_pairs(early, 1, ahead)
+    for j in range(1, ahead):
+        start_pairs(leading, j + 1, min(j + 2, pairs))
+        start_pairs(early, j, j + 1)
     start_pairs(far, 1, far_ahead)
     start_pairs(handed, 1, handed_ahead)
 
@@ -490,6 +494,7 @@
             return 0
 
         lax.fori_loop(1, peers, start_z, 0)
+        start_pairs(leading, min(ahead + 1, pairs), pairs)
         start_pairs(early, ahead, pairs)
         start_pairs(calm, ahead, pairs)
         rnum[my_peer] = snum[my_peer]
@@ -640,7 +645,7 @@
             stored(moved_chunk(j)).start()
 
     def finish(j):
-        for sends in (early, calm, far, handed, slow, late):
+        for sends in (leading, early, calm, far, handed, slow, late):
             send_pair(sends, j, wait_send)
         send_pair(onward, j, wait_send)
         for o in range(2):
@@ -741,6 +746,22 @@
         @pl.when(is_a)
         def _():
             far_bias_copy().wait_send()
+
+
+def hand_over(video_ref, text_ref, video_out, text_out, video_part, text_part, sem):
+    rows = video_ref.shape[0] // PARTS
+    parts = [pl.ds(i * rows, rows) for i in range(PARTS)]
+    into = [pltpu.make_async_copy(video_ref.at[p], video_part.at[p], sem.at[0, i]) for i, p in enumerate(parts)]
+    onto = [pltpu.make_async_copy(video_part.at[p], video_out.at[p], sem.at[1, i]) for i, p in enumerate(parts)]
+    into.append(pltpu.make_async_copy(text_ref, text_part, sem.at[0, PARTS]))
+    onto.append(pltpu.make_async_copy(text_part, text_out, sem.at[1, PARTS]))
+    for copy in into:
+        copy.start()
+    for first, second in zip(into, onto):
+        first.wait()
+        second.start()
+    for copy in onto:
+        copy.wait()
 
 
 def per_device(video_q, video_k, video_v, text_q, text_k, text_v, window, counts, text_count):
@@ -814,7 +835,20 @@
             collective_id=0, has_side_effects=True, vmem_limit_bytes=56 * 1024 * 1024
         ),
     )(video_q, video_k, video_v, text_q, text_k, text_v, window, counts, text_count)
-    return (video_out, text_out)
+    return pl.pallas_call(
+        hand_over,
+        out_shape=(
+            jax.ShapeDtypeStruct((tokens, width), bf16),
+            jax.ShapeDtypeStruct((share, width), bf16),
+        ),
+        in_specs=[hbm] * 2,
+        out_specs=(hbm, hbm),
+        scratch_shapes=[
+            pltpu.VMEM((tokens, width), bf16),
+            pltpu.VMEM((share, width), bf16),
+            dma((2, PARTS + 1)),
+        ],
+    )(video_out, text_out)
 
 
 def solution(mesh):

time: 136 us -> 135 us (level)
  local copies, waits for them, and re-layouts: 3.33 us -> 0 us
  Pallas kernels: 130 us -> 132 us
    unnamed x4 -> x0, local copies, waits for them, and re-layouts: 3.33 us -> none
    pallas_call x0 -> x1, Pallas kernels: none -> 2.34 us  [per_device(): pl.pallas_call(hand_over, out_shape=(jax.ShapeDtypeStruct((tokens, width)...]
where the time goes in v4:
time: 135 us; the launch traced here: 134 us
  Pallas kernels  132 us (98%)
    pallas_call x1, Pallas kernels, per_device(): pl.pallas_call(functools.partial(main_kernel, n, fold), out_shape=(jax.Sh...  130 us

profile of v4, /device:TPU:24, one launch (start us, length us, event | category | flops | bytes accessed | tf_op | source)
XLA Modules:
  0.0 133.6 jit_solution(13700250723462580546)
XLA Ops:
  1.3 130.0 %shard_map.104 = (bf16[256,3072]{1,0:T(8,128)(2,1)}, bf16[16,3072]{1,0:T(8,128)(2,1)}) custom-call(bf16[256,3072]{1,0:T(8,128)(2,1)} %q_hbm.1, bf16[256,3072]{1,0:T(8,128)(2,1)} %k_hbm.1, bf16[256,3072]{1,0:T(8,128)(2,1)} %v_hbm.1, bf16[256,3072]{1,0:T(8,128)(2,1)} %tq_hbm.1, bf16[256,3072]{1,0:T(8,128)(2,1)} %tk_hbm.1, bf16[256,3072]{1,0:T(8,128)(2,1)} %tv_hbm.1, ...), custom_call_target="tpu_custom_call" | custom-call | tf_op jit(solution)/shard_map/pallas_call | solution.py:781
  131.3 2.3 %shard_map.105 = (bf16[256,3072]{1,0:T(8,128)(2,1)}, bf16[16,3072]{1,0:T(8,128)(2,1)}) custom-call(bf16[256,3072]{1,0:T(8,128)(2,1)} %get-tuple-element.4.video_ref, bf16[16,3072]{1,0:T(8,128)(2,1)} %get-tuple-element.5.text_ref), custom_call_target="tpu_custom_call" | custom-call | tf_op jit(solution)/shard_map/pallas_call | solution.py:838

commit v5 on v4

--- a/solution.py
+++ b/solution.py
@@ -45,7 +45,7 @@
     out_ref, tout_ref, q_ref, k_ref, v_ref, tq_ref, tk_ref, tv_ref,
     own_ref, bias_ref, qv_ref, near, near_bias,
     relay, far_bias, far_q, side, far_out, back,
-    tnum, tstat, ynum, ystat, snum, sstat, rnum, rstat,
+    tnum, tstat, ynum, ystat, snum, sstat, rnum, rstat, fnum,
     load_sem, send_sem, recv_sem, bsend_sem, brecv_sem, fsend_sem, hsend_sem, rsend_sem, rrecv_sem,
     qsend_sem, qrecv_sem, xsend_sem, xrecv_sem, osend_sem, orecv_sem,
     ysend_sem, yrecv_sem, zsend_sem, zrecv_sem, store_sem,
@@ -469,6 +469,11 @@
             remote(sstat.at[source], rstat.at[target], zsend_sem.at[1, i], zrecv_sem.at[1, i], to),
         )
 
+    def whole_copy():
+        return remote(
+            ynum.at[my_peer + 1 - 2 * core], fnum, ysend_sem.at[2], yrecv_sem.at[2], at(1 - 2 * core)
+        )
+
     def text_exchange():
         for copy in y_copies(1 - line):
             copy.wait_recv()
@@ -483,6 +488,7 @@
             for h in range(heads):
                 cols = slice(h * HD, (h + 1) * HD)
                 num = tnum[line, k, :, cols] * one[:, h:h + 1] + ynum[k, :, cols] * two[:, h:h + 1]
+                ynum[k, :, cols] = num
                 snum[k, :, cols] = num.astype(jnp.bfloat16)
             return 0
 
@@ -493,6 +499,7 @@
                 copy.start()
             return 0
 
+        whole_copy().start()
         lax.fori_loop(1, peers, start_z, 0)
         start_pairs(leading, min(ahead + 1, pairs), pairs)
         start_pairs(early, ahead, pairs)
@@ -503,6 +510,11 @@
     row_ids = me * share + lax.broadcasted_iota(jnp.int32, (share, HD), 0)
     row_valid = row_ids < jnp.full((share, HD), tcount_ref[0], jnp.int32)
 
+    def value(i, e, cols):
+        sent = rnum[2 * i + e, :, cols].astype(jnp.float32)
+        own = jnp.where(core == e, ynum[my_peer, :, cols], fnum[:, cols])
+        return jnp.where(i == lax.div(me, 4), own, sent)
+
     def text_finish():
         def arrived(i, _):
             for copy in z_copies(i, None, None):
@@ -511,6 +523,8 @@
             return 0
 
         lax.fori_loop(1, peers, arrived, 0)
+        whole_copy().wait_send()
+        whole_copy().wait_recv()
         for e in range(2):
             top = lax.fori_loop(
                 1, peers // 2, lambda i, m: jnp.maximum(m, rstat[2 * i + e]), rstat[e]
@@ -522,8 +536,7 @@
                 scale = jnp.exp2((stat - top) * LOG2E_SCALE)
                 den = den + scale * jnp.roll(stat, 64, axis=1)
                 nums = tuple(
-                    nums[j]
-                    + rnum[2 * i + e, :, j * HD:(j + 1) * HD].astype(jnp.float32) * scale[:, j:j + 1]
+                    nums[j] + value(i, e, slice(j * HD, (j + 1) * HD)) * scale[:, j:j + 1]
                     for j in range(heads)
                 )
                 return den, nums
@@ -694,11 +707,15 @@
         def _():
             arrive(j + 1, 0)
 
+        @pl.when(j > 1)
+        def _():
+            finish(j - 2)
+
+        @pl.when(j == pairs - 1)
+        def _():
+            finish(pairs - 2)
+
         attend(j, 1)
-
-        @pl.when(j > 2)
-        def _():
-            finish(j - 3)
 
         if fold:
             pass_pair(j + passed)
@@ -741,7 +758,7 @@
         finish(j)
         return 0
 
-    lax.fori_loop(max(pairs - 3, 0), pairs, finish_rest, 0)
+    lax.fori_loop(pairs - 1, pairs, finish_rest, 0)
     if fold:
         @pl.when(is_a)
         def _():
@@ -810,6 +827,7 @@
             pltpu.VMEM((peers, share, 128), f32),
             pltpu.VMEM((peers, share, width // 2), bf16),
             pltpu.VMEM((peers, share, 128), f32),
+            pltpu.VMEM((share, width // 2), f32),
             dma((6,)),
             dma((4, 2, chunks)),
             dma((4, 2, chunks)),
@@ -825,8 +843,8 @@
             dma((2, 2, pairs)),
             dma((pairs,)),
             dma((pairs,)),
-            dma((2,)),
-            dma((2,)),
+            dma((3,)),
+            dma((3,)),
             dma((2, peers)),
             dma((2, peers)),
             dma((chunks + 1,)),

time: 135 us -> 135 us (level)
  no operation moved by 1% of the time
where the time goes in v5:
time: 135 us; the launch traced here: 133 us
  Pallas kernels  132 us (98%)
    pallas_call x1, Pallas kernels, per_device(): pl.pallas_call(functools.partial(main_kernel, n, fold), out_shape=(jax.Sh...  130 us

profile of v5, /device:TPU:24, one launch (start us, length us, event | category | flops | bytes accessed | tf_op | source)
XLA Modules:
  0.0 133.3 jit_solution(6879911995223880530)
XLA Ops:
  1.3 129.7 %shard_map.104 = (bf16[256,3072]{1,0:T(8,128)(2,1)}, bf16[16,3072]{1,0:T(8,128)(2,1)}) custom-call(bf16[256,3072]{1,0:T(8,128)(2,1)} %q_hbm.1, bf16[256,3072]{1,0:T(8,128)(2,1)} %k_hbm.1, bf16[256,3072]{1,0:T(8,128)(2,1)} %v_hbm.1, bf16[256,3072]{1,0:T(8,128)(2,1)} %tq_hbm.1, bf16[256,3072]{1,0:T(8,128)(2,1)} %tk_hbm.1, bf16[256,3072]{1,0:T(8,128)(2,1)} %tv_hbm.1, ...), custom_call_target="tpu_custom_call" | custom-call | tf_op jit(solution)/shard_map/pallas_call | solution.py:798
  131.0 2.3 %shard_map.105 = (bf16[256,3072]{1,0:T(8,128)(2,1)}, bf16[16,3072]{1,0:T(8,128)(2,1)}) custom-call(bf16[256,3072]{1,0:T(8,128)(2,1)} %get-tuple-element.4.video_ref, bf16[16,3072]{1,0:T(8,128)(2,1)} %get-tuple-element.5.text_ref), custom_call_target="tpu_custom_call" | custom-call | tf_op jit(solution)/shard_map/pallas_call | solution.py:856

commit v6 on v5

--- a/solution.py
+++ b/solution.py
@@ -213,12 +213,16 @@
             (from_relay, 3, me == 2, both, every),
             (from_relay, 0, me == n - 2, (0,), relayed),
         ]
+    paced = (row == NR - 1) | is_e if fold else row == NR - 1
     early = [
-        (direct, 0, plain_next, both, every),
-        (direct, 1, plain_prev & (row < NR - 1), both, every),
+        (direct, 0, plain_next & (row > 0), both, every),
+        (direct, 1, plain_prev & off(paced), both, every),
         (direct, 2, plain_down, both, every),
     ]
-    calm = [(direct, 1, plain_prev & (row == NR - 1), both, every)]
+    calm = [
+        (direct, 1, plain_prev & paced, both, every),
+        (direct, 0, plain_next & (row == 0), both, every),
+    ]
     late = [(direct, 3, (row == 2) & (time == 0), both, every)]
     carries = (row == 2) & (time < last)
     forwards = [(0, (row == 1) & (time > 0)), (1, carries & off(is_c) if fold else carries)]
@@ -452,7 +456,7 @@
     for copy in y_copies(1 - line):
         copy.start()
     start_pairs(handed, handed_ahead, pairs)
-    start_pairs(calm, 0, ahead)
+    start_pairs(calm, 0, min(1, pairs))
     start_pairs(late, 0, 1)
 
     peers = n // 2
@@ -503,7 +507,6 @@
         lax.fori_loop(1, peers, start_z, 0)
         start_pairs(leading, min(ahead + 1, pairs), pairs)
         start_pairs(early, ahead, pairs)
-        start_pairs(calm, ahead, pairs)
         rnum[my_peer] = snum[my_peer]
         rstat[my_peer] = sstat[my_peer]
 
@@ -594,34 +597,6 @@
 
     def attend(j, o):
         c = 2 * j + o
-        skip = is_a & moved[o](j) if fold else None
-        awaited = [
-            (0, has[0] & off(hands0)), (1, has[1] & off(hands1)),
-            (2, has[2] & even), (3, has[3] & odd & off(is_e) if fold else has[3] & odd),
-        ]
-        for d, condition in awaited:
-            @pl.when(condition if skip is None or d % 2 else condition & off(skip))
-            def _(d=d):
-                direct(d, 0, c).wait_recv()
-                direct(d, 1, c).wait_recv()
-
-        def mine():
-            for h in range(PER):
-                cols = pl.ds(pl.multiple_of(c * WIDTH + h * HD, HD), HD)
-                here = slice(h * HD, (h + 1) * HD)
-                blocks = [(k_ref[:, cols], v_ref[:, cols], bias_ref.at[0])]
-                for d in range(4):
-                    blocks.append((near[d, 0, c, :, here], near[d, 1, c, :, here], bias_ref.at[d + 1]))
-                blocks.append((tk_ref[:, cols], tv_ref[:, cols], bias_ref.at[5]))
-                result = softmax_block(q_ref[:, cols], blocks, half)
-                out_ref[:, cols] = jnp.where(qv_ref[...] > 0, result, 0.0).astype(jnp.bfloat16)
-            stored(c).start()
-
-        if skip is None:
-            mine()
-        else:
-            pl.when(off(skip))(mine)
-
         if fold:
             @pl.when(is_e & moved[o](j))
             def _(i=j + o):
@@ -646,6 +621,34 @@
                     result = softmax_block(far_q[i, :, here], blocks, half)
                     far_out[i, :, here] = result.astype(jnp.bfloat16)
                 out_copy(i).start()
+
+        skip = is_a & moved[o](j) if fold else None
+        awaited = [
+            (0, has[0] & off(hands0)), (1, has[1] & off(hands1)),
+            (2, has[2] & even), (3, has[3] & odd & off(is_e) if fold else has[3] & odd),
+        ]
+        for d, condition in awaited:
+            @pl.when(condition if skip is None or d % 2 else condition & off(skip))
+            def _(d=d):
+                direct(d, 0, c).wait_recv()
+                direct(d, 1, c).wait_recv()
+
+        def mine():
+            for h in range(PER):
+                cols = pl.ds(pl.multiple_of(c * WIDTH + h * HD, HD), HD)
+                here = slice(h * HD, (h + 1) * HD)
+                blocks = [(k_ref[:, cols], v_ref[:, cols], bias_ref.at[0])]
+                for d in range(4):
+                    blocks.append((near[d, 0, c, :, here], near[d, 1, c, :, here], bias_ref.at[d + 1]))
+                blocks.append((tk_ref[:, cols], tv_ref[:, cols], bias_ref.at[5]))
+                result = softmax_block(q_ref[:, cols], blocks, half)
+                out_ref[:, cols] = jnp.where(qv_ref[...] > 0, result, 0.0).astype(jnp.bfloat16)
+            stored(c).start()
+
+        if skip is None:
+            mine()
+        else:
+            pl.when(off(skip))(mine)
 
     def take(j):
         @pl.when(is_a)
@@ -695,6 +698,10 @@
             @pl.when(j + far_ahead < pairs)
             def _():
                 send_pair(far, j + far_ahead, start)
+
+        @pl.when(j + 1 < pairs)
+        def _():
+            send_pair(calm, j + 1, start)
 
         @pl.when(j + 1 < pairs)
         def _():

time: 135 us -> 133 us (0.985); the launches traced: 133 us -> 133 us
  no operation moved by 1% of the time
where the time goes in v6:
time: 133 us
  Pallas kernels  132 us (99%)
    pallas_call x1, Pallas kernels, per_device(): pl.pallas_call(functools.partial(main_kernel, n, fold), out_shape=(jax.Sh...  129 us

profile of v6, /device:TPU:24, one launch (start us, length us, event | category | flops | bytes accessed | tf_op | source)
XLA Modules:
  0.0 133.1 jit_solution(1089274664263792767)
XLA Ops:
  1.3 129.4 %shard_map.104 = (bf16[256,3072]{1,0:T(8,128)(2,1)}, bf16[16,3072]{1,0:T(8,128)(2,1)}) custom-call(bf16[256,3072]{1,0:T(8,128)(2,1)} %q_hbm.1, bf16[256,3072]{1,0:T(8,128)(2,1)} %k_hbm.1, bf16[256,3072]{1,0:T(8,128)(2,1)} %v_hbm.1, bf16[256,3072]{1,0:T(8,128)(2,1)} %tq_hbm.1, bf16[256,3072]{1,0:T(8,128)(2,1)} %tk_hbm.1, bf16[256,3072]{1,0:T(8,128)(2,1)} %tv_hbm.1, ...), custom_call_target="tpu_custom_call" | custom-call | tf_op jit(solution)/shard_map/pallas_call | solution.py:805
  130.7 2.3 %shard_map.105 = (bf16[256,3072]{1,0:T(8,128)(2,1)}, bf16[16,3072]{1,0:T(8,128)(2,1)}) custom-call(bf16[256,3072]{1,0:T(8,128)(2,1)} %get-tuple-element.4.video_ref, bf16[16,3072]{1,0:T(8,128)(2,1)} %get-tuple-element.5.text_ref), custom_call_target="tpu_custom_call" | custom-call | tf_op jit(solution)/shard_map/pallas_call | solution.py:863

commit v7 on v6

--- a/solution.py
+++ b/solution.py
@@ -12,7 +12,7 @@
 NR = 4
 WIDTH = 256
 PER = WIDTH // HD
-AHEAD = 5
+AHEAD = 4
 PARTS = 8
 LOG2E_SCALE = math.log2(math.e) / math.sqrt(HD)
 MESH = pl.DeviceIdType.MESH

time: 133 us -> 133 us (level)
  no operation moved by 1% of the time
where the time goes in v7:
time: 133 us
  Pallas kernels  132 us (99%)
    pallas_call x1, Pallas kernels, per_device(): pl.pallas_call(functools.partial(main_kernel, n, fold), out_shape=(jax.Sh...  129 us

profile of v7, /device:TPU:24, one launch (start us, length us, event | category | flops | bytes accessed | tf_op | source)
XLA Modules:
  0.0 133.1 jit_solution(4434194742373886641)
XLA Ops:
  1.3 129.4 %shard_map.104 = (bf16[256,3072]{1,0:T(8,128)(2,1)}, bf16[16,3072]{1,0:T(8,128)(2,1)}) custom-call(bf16[256,3072]{1,0:T(8,128)(2,1)} %q_hbm.1, bf16[256,3072]{1,0:T(8,128)(2,1)} %k_hbm.1, bf16[256,3072]{1,0:T(8,128)(2,1)} %v_hbm.1, bf16[256,3072]{1,0:T(8,128)(2,1)} %tq_hbm.1, bf16[256,3072]{1,0:T(8,128)(2,1)} %tk_hbm.1, bf16[256,3072]{1,0:T(8,128)(2,1)} %tv_hbm.1, ...), custom_call_target="tpu_custom_call" | custom-call | tf_op jit(solution)/shard_map/pallas_call | solution.py:805
  130.7 2.3 %shard_map.105 = (bf16[256,3072]{1,0:T(8,128)(2,1)}, bf16[16,3072]{1,0:T(8,128)(2,1)}) custom-call(bf16[256,3072]{1,0:T(8,128)(2,1)} %get-tuple-element.4.video_ref, bf16[16,3072]{1,0:T(8,128)(2,1)} %get-tuple-element.5.text_ref), custom_call_target="tpu_custom_call" | custom-call | tf_op jit(solution)/shard_map/pallas_call | solution.py:863
